TPU v7x, 512 devices: a whole 4x4x16 slice. The times are simulated.
512 devices in a mesh: node: 32 (over y, x, core), period: 16 (over z).
Axes of the slice: x: 4, y: 4, z: 16, core: 2. Of those that a mesh axis runs over, the one named last changes fastest.
Arguments:
- prod_start: float32 [128, 131072], P('period', 'node'), may hold values from 0 to 1
- flow_inner_start: float32 [128, 655360], P('period', 'node'), may hold values from 0 to 1
- flow_cut_start: float32 [128, 131072], P('period', 'node'), may hold values from 0 to 1
- dual_start: float32 [128, 131072], P('period', 'node'), may hold values from -6 to 6
- cost_prod: float32 [128, 131072], P('period', 'node'), may hold values from 0.02 to 14
- cost_inner: float32 [128, 655360], P('period', 'node'), may hold values from 0.02 to 14
- cost_cut: float32 [128, 131072], P('period', 'node'), may hold values from 0.02 to 14
- inv_target: float32 [128, 131072], P('period', 'node'), may hold values from 0.04 to 27
- keep: float32 [128, 131072], P('period', 'node'), may hold values from 0.45 to 1
- inner_tail: int32 [655360], P('node'), may hold values from 0 to 4095, as said below
- inner_head: int32 [655360], P('node'), may hold values from 0 to 4095, as said below
- cut_tail: int32 [131072], P('node'), may hold values from 0 to 4095, as said below
- cut_head: int32 [131072], P('node'), may hold values from 0 to 4095, as said below
Outputs:
- prod_final: float32 [128, 131072], P('period', 'node')
- flow_inner_final: float32 [128, 655360], P('period', 'node')
- flow_cut_final: float32 [128, 131072], P('period', 'node')
- dual_final: float32 [128, 131072], P('period', 'node')
Inputs may be any that keep to these rules, and one draw needn't show every extreme that they name: `inner_tail`: inner arcs come in aligned blocks of 128 within a slab; with j the block's number within its slab, R = 32, the tails of block j are the nodes of tile j % R (nodes (j % R) * 128 to (j % R) * 128 + 127), each once. `inner_head`: the heads of inner arc block j are the nodes of tile (j % R + j // R) % R, each once, with R = 32. `cut_tail`: cut tails of the entries m to m + 127 of a slab's list, m a multiple of 128, are the nodes m to m + 127 of the slab, each once. `cut_head`: cut heads of the entries m to m + 127 of a slab's list, m a multiple of 128, are the nodes m to m + 127 of the slab, each once.
All inputs are finite; a program needn't handle non-finite values.
Results may differ from a plain program's by a relative error of at most 0.00012.
Values sent between devices are 32-bit elements; how exact they have to be, the bound alone decides.
A program may use at most 64 MiB of HBM per device.

v0:
```python
import math

import jax
import jax.numpy as jnp
from jax import lax
from jax.sharding import PartitionSpec as P

ITERS = 2
TILE = 128


ETA = 0.25


def chain(values, decay):
    count, columns = values.shape
    block = math.gcd(count, 16)
    blocks = count // block
    folded = values.reshape(blocks, block, columns).transpose(1, 0, 2)
    kept = decay.reshape(blocks, block, columns).transpose(1, 0, 2)

    def advance(carry, pair):
        value, factor = pair
        carry = factor * carry + value
        return (carry, carry)

    _, local = lax.scan(advance, jnp.zeros((blocks, columns), jnp.float32), (folded, kept))
    products = jnp.cumprod(kept, axis=0)

    def across(carry, pair):
        factor, value = pair
        return (factor * carry + value, carry)

    _, entering = lax.scan(across, jnp.zeros((columns,), jnp.float32), (products[-1], local[-1]))
    local = local + products * entering[None]
    return local.transpose(1, 0, 2).reshape(count, columns)


def one_hot_tiles(offsets):
    tiles = offsets.shape[0] // TILE
    within = (offsets % TILE).reshape(tiles, TILE)
    return (within[:, :, None] == lax.iota(jnp.int32, TILE)[None, None, :]).astype(jnp.float32)


def spread_tiles(values, table):
    return jnp.einsum("pta,tan->ptn", values, table, precision=lax.Precision.HIGHEST)


def pick_tiles(values, table):
    return jnp.einsum("ptn,tan->pta", values, table, precision=lax.Precision.HIGHEST)


def body(
    prod_start,
    flow_inner_start,
    flow_cut_start,
    dual_start,
    cost_prod,
    cost_inner,
    cost_cut,
    inv_target,
    keep,
    inner_tail,
    inner_head,
    cut_tail,
    cut_head,
):
    row_count, slab_width = prod_start.shape
    tile_count = slab_width // TILE
    groups = inner_tail.shape[0] // slab_width
    horizon = row_count * lax.axis_size("period")
    local_costs = (
        jnp.sum(cost_prod * cost_prod)
        + jnp.sum(cost_inner * cost_inner)
        + jnp.sum(cost_cut * cost_cut)
    )
    local_targets = jnp.sum(inv_target * inv_target)
    cost_squares, target_squares = lax.psum((local_costs, local_targets), ("node", "period"))
    omega = jnp.sqrt(cost_squares / target_squares)
    tau = ETA / omega
    sigma = ETA * omega
    keep_nodes = lax.all_to_all(keep, "period", split_axis=1, concat_axis=0, tiled=True)
    later_nodes = jnp.concatenate([keep_nodes[1:], jnp.zeros_like(keep_nodes[:1])], axis=0)

    def tiled(values):
        return values.reshape(row_count, tile_count, TILE)

    def inner_group(index_list, group):
        return one_hot_tiles(
            lax.slice_in_dim(index_list, group * slab_width, (group + 1) * slab_width)
        )

    def inner_net(inner_flow):
        grouped = inner_flow.reshape(row_count, groups, tile_count, TILE)
        total = jnp.zeros((row_count, tile_count, TILE), jnp.float32)
        for group in range(groups):
            arrived = spread_tiles(grouped[:, group], inner_group(inner_head, group))
            left = spread_tiles(grouped[:, group], inner_group(inner_tail, group))
            total = total + jnp.roll(arrived, group, axis=1) - left
        return total.reshape(row_count, slab_width)

    def inner_prices(price):
        blocked = tiled(price)
        pieces = []
        for group in range(groups):
            at_head = pick_tiles(jnp.roll(blocked, -group, axis=1), inner_group(inner_head, group))
            at_tail = pick_tiles(blocked, inner_group(inner_tail, group))
            pieces.append(at_head - at_tail)
        return jnp.stack(pieces, axis=1).reshape(row_count, groups * slab_width)

    produced, inner_flow, cut_flow, dual = (
        prod_start,
        flow_inner_start,
        flow_cut_start,
        dual_start,
    )
    for sweep in range(ITERS):
        dual_nodes = lax.all_to_all(dual, "period", split_axis=1, concat_axis=0, tiled=True)
        accumulated = chain(dual_nodes[::-1], later_nodes[::-1])[::-1]
        price = (
            lax.all_to_all(accumulated, "period", split_axis=0, concat_axis=1, tiled=True) / horizon
        )
        head_price = pick_tiles(tiled(price), one_hot_tiles(cut_head)).reshape(
            row_count, slab_width
        )
        returned = lax.all_to_all(head_price, "node", split_axis=1, concat_axis=1, tiled=True)
        tail_price = pick_tiles(tiled(price), one_hot_tiles(cut_tail)).reshape(
            row_count, slab_width
        )
        inner_price = inner_prices(price)
        cut_price = returned - tail_price
        new_prod = jnp.maximum(produced - tau * (cost_prod - price), 0.0)
        new_inner = jnp.maximum(inner_flow - tau * (cost_inner - inner_price), 0.0)
        new_cut = jnp.maximum(cut_flow - tau * (cost_cut - cut_price), 0.0)
        balance_produced = 2.0 * new_prod - produced
        balance_inner_flow = 2.0 * new_inner - inner_flow
        balance_cut_flow = 2.0 * new_cut - cut_flow
        balance_arrived = lax.all_to_all(
            balance_cut_flow, "node", split_axis=1, concat_axis=1, tiled=True
        )
        net = balance_produced + inner_net(balance_inner_flow)
        balance_left = spread_tiles(tiled(balance_cut_flow), one_hot_tiles(cut_tail)).reshape(
            row_count, slab_width
        )
        entered = spread_tiles(tiled(balance_arrived), one_hot_tiles(cut_head)).reshape(
            row_count, slab_width
        )
        net = net - balance_left + entered
        net_nodes = lax.all_to_all(net, "period", split_axis=1, concat_axis=0, tiled=True)
        stock = chain(net_nodes, keep_nodes)
        dual = dual + sigma * (
            inv_target
            - lax.all_to_all(stock, "period", split_axis=0, concat_axis=1, tiled=True) / horizon
        )
        produced, inner_flow, cut_flow = (new_prod, new_inner, new_cut)
    return (produced, inner_flow, cut_flow, dual)


def solution(mesh):
    return jax.shard_map(
        body,
        mesh=mesh,
        in_specs=(
            P("period", "node"),
            P("period", "node"),
            P("period", "node"),
            P("period", "node"),
            P("period", "node"),
            P("period", "node"),
            P("period", "node"),
            P("period", "node"),
            P("period", "node"),
            P("node"),
            P("node"),
            P("node"),
            P("node"),
        ),
        out_specs=(
            P("period", "node"),
            P("period", "node"),
            P("period", "node"),
            P("period", "node"),
        ),
        check_vma=False,
    )
```

profile of v0, /device:TPU:1, one launch (start us, length us, event | category | flops | bytes accessed | tf_op | source)
XLA Modules:
  0.0 423.0 jit_solution(738403177668012609)
XLA Ops:
  0.6 15.8 %all-to-all-start = ((f32[8,16,256]{2,0,1:T(8,128)}), f32[8,16,256]{2,0,1:T(8,128)S(1)}, u32[]{:S(2)}, u32[]{:S(2)}) async-start(f32[8,16,256]{2,0,1:T(8,128)} %bitcast.576), calls=%async_computation | async-start | bytes 262144 | tf_op jit(solution)/shard_map/all_to_all | solution.py:82
  19.6 1.9 multiply_reduce_fusion
  21.4 7.0 %all-to-all-done = f32[8,16,256]{2,0,1:T(8,128)S(1)} async-done(((f32[8,16,256]{2,0,1:T(8,128)}), f32[8,16,256]{2,0,1:T(8,128)S(1)}, u32[]{:S(2)}, u32[]{:S(2)}) %all-to-all-start) | async-done | bytes 131104 | tf_op jit(solution)/shard_map/all_to_all | solution.py:82
  28.4 5.9 %all-to-all-start.1 = ((f32[8,16,256]{2,0,1:T(8,128)}), f32[8,16,256]{2,0,1:T(8,128)S(1)}, u32[]{:S(2)}, u32[]{:S(2)}) async-start(f32[8,16,256]{2,0,1:T(8,128)} %bitcast.5), calls=%async_computation.1 | async-start | bytes 262144 | tf_op jit(solution)/shard_map/all_to_all | solution.py:118
  37.3 9.0 %all-to-all-done.1 = f32[8,16,256]{2,0,1:T(8,128)S(1)} async-done(((f32[8,16,256]{2,0,1:T(8,128)}), f32[8,16,256]{2,0,1:T(8,128)S(1)}, u32[]{:S(2)}, u32[]{:S(2)}) %all-to-all-start.1) | async-done | bytes 131104 | tf_op jit(solution)/shard_map/all_to_all | solution.py:118
  49.0 5.5 %all-to-all-start.2 = ((f32[16,8,256]{2,1,0:T(8,128)}), f32[16,8,256]{2,1,0:T(8,128)S(1)}, u32[]{:S(2)}, u32[]{:S(2)}) async-start(f32[16,8,256]{2,1,0:T(8,128)} %bitcast.15), calls=%async_computation.2 | async-start | bytes 262144 | tf_op jit(solution)/shard_map/all_to_all | solution.py:121
  55.1 105.9 %all-reduce.1 = (f32[]{:T(128)}, f32[]{:T(128)}) all-reduce(f32[]{:T(128)S(6)} %add.257, f32[]{:T(128)} %multiply_reduce_fusion.1), channel_id=1, replica_groups=mesh['node'=32,'period'=16] {'node','period'}, use_global_device_ids=true, to_apply=%region_3.0 | all-reduce | flops 2 | bytes 16 | tf_op jit(solution)/shard_map/psum | solution.py:78
  162.8 2.4 fusion.47
  165.2 2.4 fusion.39
  167.6 2.4 fusion.31
  170.0 2.4 fusion.23
  172.3 2.4 fusion.15
  174.7 2.4 fusion.104
  177.1 1.8 fusion.116
  184.5 1.8 fusion.52
  186.4 2.1 fusion.46
  188.5 1.8 fusion.56
  190.3 1.8 fusion.60
  192.2 1.8 fusion.64
  194.1 2.6 fusion.70
  196.8 4.4 %all-to-all-start.3 = ((f32[8,32,128]{2,0,1:T(8,128)}), f32[8,32,128]{2,0,1:T(8,128)S(1)}, u32[]{:S(2)}, u32[]{:S(2)}) async-start(f32[8,32,128]{2,0,1:T(8,128)} %fusion.70), calls=%async_computation.3 | async-start | bytes 262144 | tf_op jit(solution)/shard_map/all_to_all | solution.py:126
  201.3 2.3 fusion.107
  203.7 1.8 fusion.101
  205.6 1.8 fusion.97
  207.5 2.1 fusion.93
  209.6 3.2 fusion.83
  213.4 7.5 %all-to-all-start.4 = ((f32[8,32,128]{2,0,1:T(8,128)}), f32[8,32,128]{2,0,1:T(8,128)S(1)}, u32[]{:S(2)}, u32[]{:S(2)}) async-start(f32[8,32,128]{2,0,1:T(8,128)} %subtract_bitcast_fusion.1), calls=%async_computation.4 | async-start | bytes 262144 | tf_op jit(solution)/shard_map/all_to_all | solution.py:138
  220.9 2.3 fusion.89
  223.3 5.3 %all-to-all-done.4 = f32[8,32,128]{2,0,1:T(8,128)S(1)} async-done(((f32[8,32,128]{2,0,1:T(8,128)}), f32[8,32,128]{2,0,1:T(8,128)S(1)}, u32[]{:S(2)}, u32[]{:S(2)}) %all-to-all-start.4) | async-done | bytes 131104 | tf_op jit(solution)/shard_map/all_to_all | solution.py:138
  228.6 1.8 convolution_bitcast_fusion.2
  230.4 2.8 fusion.5
  233.2 8.5 %all-to-all-start.5 = ((f32[8,16,256]{2,0,1:T(8,128)}), f32[8,16,256]{2,0,1:T(8,128)S(1)}, u32[]{:S(2)}, u32[]{:S(2)}) async-start(f32[8,16,256]{2,0,1:T(8,128)} %bitcast.69), calls=%async_computation.5 | async-start | bytes 262144 | tf_op jit(solution)/shard_map/all_to_all | solution.py:149
  242.0 11.9 %all-to-all-done.5 = f32[8,16,256]{2,0,1:T(8,128)S(1)} async-done(((f32[8,16,256]{2,0,1:T(8,128)}), f32[8,16,256]{2,0,1:T(8,128)S(1)}, u32[]{:S(2)}, u32[]{:S(2)}) %all-to-all-start.5) | async-done | bytes 131104 | tf_op jit(solution)/shard_map/all_to_all | solution.py:149
  256.4 6.5 %all-to-all-start.6 = ((f32[16,8,256]{2,1,0:T(8,128)}), f32[16,8,256]{2,1,0:T(8,128)S(1)}, u32[]{:S(2)}, u32[]{:S(2)}) async-start(f32[16,8,256]{2,1,0:T(8,128)} %bitcast.78), calls=%async_computation.6 | async-start | bytes 262144 | tf_op jit(solution)/shard_map/all_to_all | solution.py:153
  262.9 12.0 %all-to-all-done.6 = f32[16,8,256]{2,1,0:T(8,128)S(1)} async-done(((f32[16,8,256]{2,1,0:T(8,128)}), f32[16,8,256]{2,1,0:T(8,128)S(1)}, u32[]{:S(2)}, u32[]{:S(2)}) %all-to-all-start.6) | async-done | bytes 131104 | tf_op jit(solution)/shard_map/all_to_all | solution.py:153
  276.5 6.0 %all-to-all-start.7 = ((f32[8,16,256]{2,0,1:T(8,128)}), f32[8,16,256]{2,0,1:T(8,128)S(1)}, u32[]{:S(2)}, u32[]{:S(2)}) async-start(f32[8,16,256]{2,0,1:T(8,128)} %bitcast.81), calls=%async_computation.7 | async-start | bytes 262144 | tf_op jit(solution)/shard_map/all_to_all | solution.py:118
  282.5 12.0 %all-to-all-done.7 = f32[8,16,256]{2,0,1:T(8,128)S(1)} async-done(((f32[8,16,256]{2,0,1:T(8,128)}), f32[8,16,256]{2,0,1:T(8,128)S(1)}, u32[]{:S(2)}, u32[]{:S(2)}) %all-to-all-start.7) | async-done | bytes 131104 | tf_op jit(solution)/shard_map/all_to_all | solution.py:118
  296.5 17.3 %all_to_all.165 = f32[16,8,256]{2,1,0:T(8,128)S(1)} all-to-all(f32[16,8,256]{2,1,0:T(8,128)S(1)} %bitcast.570), channel_id=1, replica_groups=mesh['node'=32,'period'=16] {'period'}, dimensions={0} | all-to-all | bytes 262144 | tf_op jit(solution)/shard_map/all_to_all | solution.py:121
  313.7 2.4 fusion.45
  316.1 2.4 fusion.37
  318.6 2.4 fusion.29
  321.0 2.4 fusion.21
  323.4 2.4 fusion.13
  325.9 2.4 fusion.110
  328.2 1.8 fusion.119
  336.5 1.8 fusion.53
  338.3 1.8 fusion.44
  340.2 1.8 fusion.57
  342.0 1.8 fusion.61
  343.8 1.8 fusion.65
  345.7 2.6 fusion.71
  348.4 7.5 %all-to-all-start.9 = ((f32[8,32,128]{2,0,1:T(8,128)}), f32[8,32,128]{2,0,1:T(8,128)S(1)}, u32[]{:S(2)}, u32[]{:S(2)}) async-start(f32[8,32,128]{2,0,1:T(8,128)} %fusion.71), calls=%async_computation.9 | async-start | bytes 262144 | tf_op jit(solution)/shard_map/all_to_all | solution.py:126
  356.0 1.8 fusion.113
  357.9 1.8 fusion.99
  359.8 1.8 fusion.95
  363.7 2.4 fusion.77
  366.8 6.7 %all-to-all-start.10 = ((f32[8,32,128]{2,0,1:T(8,128)}), f32[8,32,128]{2,0,1:T(8,128)S(1)}, u32[]{:S(2)}, u32[]{:S(2)}) async-start(f32[8,32,128]{2,0,1:T(8,128)} %subtract_bitcast_fusion), calls=%async_computation.10 | async-start | bytes 262144 | tf_op jit(solution)/shard_map/all_to_all | solution.py:138
  373.5 1.8 fusion.86
  375.4 5.8 %all-to-all-done.10 = f32[8,32,128]{2,0,1:T(8,128)S(1)} async-done(((f32[8,32,128]{2,0,1:T(8,128)}), f32[8,32,128]{2,0,1:T(8,128)S(1)}, u32[]{:S(2)}, u32[]{:S(2)}) %all-to-all-start.10) | async-done | bytes 131104 | tf_op jit(solution)/shard_map/all_to_all | solution.py:138
  381.1 1.8 convolution_bitcast_fusion
  383.0 2.8 fusion.7
  385.8 3.5 all-to-all-start.11
  389.3 12.0 %all-to-all-done.11 = f32[8,16,256]{2,0,1:T(8,128)S(1)} async-done(((f32[8,16,256]{2,0,1:T(8,128)}), f32[8,16,256]{2,0,1:T(8,128)S(1)}, u32[]{:S(2)}, u32[]{:S(2)}) %all-to-all-start.11) | async-done | bytes 131104 | tf_op jit(solution)/shard_map/all_to_all | solution.py:149
  403.2 18.2 %all_to_all.166 = f32[16,8,256]{2,1,0:T(8,128)S(1)} all-to-all(f32[16,8,256]{2,1,0:T(8,128)S(1)} %bitcast.571), channel_id=1, replica_groups=mesh['node'=32,'period'=16] {'period'}, dimensions={0} | all-to-all | bytes 262144 | tf_op jit(solution)/shard_map/all_to_all | solution.py:153
  (445 shorter events, 36.7 us)
Async XLA Ops:
  0.6 27.8 %all-to-all-start = ((f32[8,16,256]{2,0,1:T(8,128)}), f32[8,16,256]{2,0,1:T(8,128)S(1)}, u32[]{:S(2)}, u32[]{:S(2)}) async-start(f32[8,16,256]{2,0,1:T(8,128)} %bitcast.576), calls=%async_computation | async-start | bytes 262144 | tf_op jit(solution)/shard_map/all_to_all | solution.py:82
  16.4 17.9 %copy-start.2 = (f32[8,4096]{1,0:T(8,128)S(1)}, f32[8,4096]{1,0:T(8,128)}, u32[]{:S(2)}) copy-start(f32[8,4096]{1,0:T(8,128)} %param.36) | copy-start | bytes 393220
  16.4 20.5 %copy-start.43 = (s32[4096]{0:T(1024)S(1)}, s32[4096]{0:T(1024)}, u32[]{:S(2)}) copy-start(s32[4096]{0:T(1024)} %param.41) | copy-start | bytes 49156
  28.4 17.9 %all-to-all-start.1 = ((f32[8,16,256]{2,0,1:T(8,128)}), f32[8,16,256]{2,0,1:T(8,128)S(1)}, u32[]{:S(2)}, u32[]{:S(2)}) async-start(f32[8,16,256]{2,0,1:T(8,128)} %bitcast.5), calls=%async_computation.1 | async-start | bytes 262144 | tf_op jit(solution)/shard_map/all_to_all | solution.py:118
  36.9 157.1 %copy-start.45 = (s32[32,128]{1,0:T(8,128)}, s32[32,128]{1,0:T(8,128)S(1)}, u32[]{:S(2)}) copy-start(s32[32,128]{1,0:T(8,128)S(1)} %fusion.223) | copy-start | bytes 49156
  48.2 6.3 %copy-start.44 = (s32[4096]{0:T(1024)S(1)}, s32[4096]{0:T(1024)}, u32[]{:S(2)}) copy-start(s32[4096]{0:T(1024)} %param.40) | copy-start | bytes 49156
  48.2 114.3 %copy-start.17 = (s32[20480]{0:T(1024)S(1)}, s32[20480]{0:T(1024)}, u32[]{:S(2)}) copy-start(s32[20480]{0:T(1024)} %param.38) | copy-start | bytes 245764
  48.2 114.3 %copy-start.18 = (s32[20480]{0:T(1024)S(1)}, s32[20480]{0:T(1024)}, u32[]{:S(2)}) copy-start(s32[20480]{0:T(1024)} %param.39) | copy-start | bytes 245764
  49.0 113.7 %all-to-all-start.2 = ((f32[16,8,256]{2,1,0:T(8,128)}), f32[16,8,256]{2,1,0:T(8,128)S(1)}, u32[]{:S(2)}, u32[]{:S(2)}) async-start(f32[16,8,256]{2,1,0:T(8,128)} %bitcast.15), calls=%async_computation.2 | async-start | bytes 262144 | tf_op jit(solution)/shard_map/all_to_all | solution.py:121
  162.5 2.7 copy-start.27
  162.5 5.0 %copy-start.24 = (s32[32,128]{1,0:T(8,128)}, s32[32,128]{1,0:T(8,128)S(1)}, u32[]{:S(2)}) copy-start(s32[32,128]{1,0:T(8,128)S(1)} %get-tuple-element.508) | copy-start | bytes 49156
  162.5 7.4 %copy-start.21 = (s32[32,128]{1,0:T(8,128)}, s32[32,128]{1,0:T(8,128)S(1)}, u32[]{:S(2)}) copy-start(s32[32,128]{1,0:T(8,128)S(1)} %get-tuple-element.511) | copy-start | bytes 49156
  162.6 9.8 %copy-start.19 = (s32[32,128]{1,0:T(8,128)}, s32[32,128]{1,0:T(8,128)S(1)}, u32[]{:S(2)}) copy-start(s32[32,128]{1,0:T(8,128)S(1)} %get-tuple-element.507) | copy-start | bytes 49156
  162.6 23.8 %copy-start.35 = (s32[32,128]{1,0:T(8,128)}, s32[32,128]{1,0:T(8,128)S(1)}, u32[]{:S(2)}) copy-start(s32[32,128]{1,0:T(8,128)S(1)} %get-tuple-element.510) | copy-start | bytes 49156
  162.6 12.1 %copy-start.30 = (s32[32,128]{1,0:T(8,128)}, s32[32,128]{1,0:T(8,128)S(1)}, u32[]{:S(2)}) copy-start(s32[32,128]{1,0:T(8,128)S(1)} %get-tuple-element.505) | copy-start | bytes 49156
  162.6 21.9 %copy-start.41 = (s32[32,128]{1,0:T(8,128)}, s32[32,128]{1,0:T(8,128)S(1)}, u32[]{:S(2)}) copy-start(s32[32,128]{1,0:T(8,128)S(1)} %get-tuple-element.504) | copy-start | bytes 49156
  162.6 25.9 %copy-start.39 = (s32[32,128]{1,0:T(8,128)}, s32[32,128]{1,0:T(8,128)S(1)}, u32[]{:S(2)}) copy-start(s32[32,128]{1,0:T(8,128)S(1)} %get-tuple-element.503) | copy-start | bytes 49156
  162.7 27.7 %copy-start.37 = (s32[32,128]{1,0:T(8,128)}, s32[32,128]{1,0:T(8,128)S(1)}, u32[]{:S(2)}) copy-start(s32[32,128]{1,0:T(8,128)S(1)} %get-tuple-element.506) | copy-start | bytes 49156
  162.7 29.5 %copy-start.33 = (s32[32,128]{1,0:T(8,128)}, s32[32,128]{1,0:T(8,128)S(1)}, u32[]{:S(2)}) copy-start(s32[32,128]{1,0:T(8,128)S(1)} %get-tuple-element.502) | copy-start | bytes 49156
  180.7 3.6 copy-start.3
  186.4 2.1 copy-start.14
  194.0 2.7 copy-start.9
  194.1 7.1 %copy-start.1 = (f32[8,4096]{1,0:T(8,128)S(1)}, f32[8,4096]{1,0:T(8,128)}, u32[]{:S(2)}) copy-start(f32[8,4096]{1,0:T(8,128)} %param.33) | copy-start | bytes 393220
  194.1 7.1 %copy-start.5 = (f32[8,4096]{1,0:T(8,128)S(1)}, f32[8,4096]{1,0:T(8,128)}, u32[]{:S(2)}) copy-start(f32[8,4096]{1,0:T(8,128)} %param.29) | copy-start | bytes 393220
  194.1 7.1 %slice-start.10 = ((f32[8,32,128]{2,0,1:T(8,128)}), f32[8,31,128]{2,0,1:T(8,128)S(1)}, s32[]{:S(2)}) async-start(f32[8,32,128]{2,0,1:T(8,128)} %copy-done.14), calls=%async_computation.23 | async-start | bytes 253952 | tf_op jit(solution)/shard_map/jit(_roll_static)/slice | solution.py:99
  194.1 7.1 %slice-start.11 = ((f32[8,32,128]{2,0,1:T(8,128)}), f32[8,1,128]{2,0,1:T(8,128)S(1)}, s32[]{:S(2)}) async-start(f32[8,32,128]{2,0,1:T(8,128)} %copy-done.14), calls=%async_computation.24 | async-start | bytes 8192 | tf_op jit(solution)/shard_map/jit(_roll_static)/slice | solution.py:99
  194.1 7.1 %copy-start.31 = (s32[32,128]{1,0:T(8,128)S(1)}, s32[32,128]{1,0:T(8,128)}, u32[]{:S(2)}) copy-start(s32[32,128]{1,0:T(8,128)} %copy-done.30) | copy-start | bytes 49156
  196.8 12.8 %all-to-all-start.3 = ((f32[8,32,128]{2,0,1:T(8,128)}), f32[8,32,128]{2,0,1:T(8,128)S(1)}, u32[]{:S(2)}, u32[]{:S(2)}) async-start(f32[8,32,128]{2,0,1:T(8,128)} %fusion.70), calls=%async_computation.3 | async-start | bytes 262144 | tf_op jit(solution)/shard_map/all_to_all | solution.py:126
  201.2 2.4 slice-start.12
  201.2 2.4 slice-start.13
  201.2 2.4 copy-start.28
  203.6 1.9 slice-start.14
  203.7 1.9 slice-start.15
  203.7 1.9 copy-start.25
  205.6 1.9 slice-start.2
  205.6 1.9 slice-start.3
  205.6 1.9 copy-start.22
  207.5 2.1 copy-start.4
  207.5 2.1 copy-start.10
  213.4 15.1 %all-to-all-start.4 = ((f32[8,32,128]{2,0,1:T(8,128)}), f32[8,32,128]{2,0,1:T(8,128)S(1)}, u32[]{:S(2)}, u32[]{:S(2)}) async-start(f32[8,32,128]{2,0,1:T(8,128)} %subtract_bitcast_fusion.1), calls=%async_computation.4 | async-start | bytes 262144 | tf_op jit(solution)/shard_map/all_to_all | solution.py:138
  220.9 7.6 %copy-start.46 = (s32[32,128]{1,0:T(8,128)S(1)}, s32[32,128]{1,0:T(8,128)}, u32[]{:S(2)}) copy-start(s32[32,128]{1,0:T(8,128)} %copy-done.45) | copy-start | bytes 49156
  223.3 7.1 %copy-start.47 = (s32[32,128]{1,0:T(8,128)S(1)}, s32[32,128]{1,0:T(8,128)}, u32[]{:S(2)}) copy-start(s32[32,128]{1,0:T(8,128)} %fusion.221) | copy-start | bytes 49156
  233.2 20.7 %all-to-all-start.5 = ((f32[8,16,256]{2,0,1:T(8,128)}), f32[8,16,256]{2,0,1:T(8,128)S(1)}, u32[]{:S(2)}, u32[]{:S(2)}) async-start(f32[8,16,256]{2,0,1:T(8,128)} %bitcast.69), calls=%async_computation.5 | async-start | bytes 262144 | tf_op jit(solution)/shard_map/all_to_all | solution.py:149
  256.4 18.5 %all-to-all-start.6 = ((f32[16,8,256]{2,1,0:T(8,128)}), f32[16,8,256]{2,1,0:T(8,128)S(1)}, u32[]{:S(2)}, u32[]{:S(2)}) async-start(f32[16,8,256]{2,1,0:T(8,128)} %bitcast.78), calls=%async_computation.6 | async-start | bytes 262144 | tf_op jit(solution)/shard_map/all_to_all | solution.py:153
  276.5 18.0 %all-to-all-start.7 = ((f32[8,16,256]{2,0,1:T(8,128)}), f32[8,16,256]{2,0,1:T(8,128)S(1)}, u32[]{:S(2)}, u32[]{:S(2)}) async-start(f32[8,16,256]{2,0,1:T(8,128)} %bitcast.81), calls=%async_computation.7 | async-start | bytes 262144 | tf_op jit(solution)/shard_map/all_to_all | solution.py:118
  296.3 17.4 %copy-start.36 = (s32[32,128]{1,0:T(8,128)S(1)}, s32[32,128]{1,0:T(8,128)}, u32[]{:S(2)}) copy-start(s32[32,128]{1,0:T(8,128)} %copy-done.35) | copy-start | bytes 49156
  313.7 2.4 copy-start.29
  316.1 2.4 copy-start.26
  318.5 2.5 copy-start.23
  321.0 2.4 copy-start.20
  323.4 2.4 copy-start.32
  325.8 2.4 copy-start.42
  345.7 2.7 copy-start.8
  345.7 10.2 %slice-start.4 = ((f32[8,32,128]{2,0,1:T(8,128)}), f32[8,31,128]{2,0,1:T(8,128)S(1)}, s32[]{:S(2)}) async-start(f32[8,32,128]{2,0,1:T(8,128)} %copy-done.11), calls=%async_computation.17 | async-start | bytes 253952 | tf_op jit(solution)/shard_map/jit(_roll_static)/slice | solution.py:99
  345.7 10.2 %slice-start.5 = ((f32[8,32,128]{2,0,1:T(8,128)}), f32[8,1,128]{2,0,1:T(8,128)S(1)}, s32[]{:S(2)}) async-start(f32[8,32,128]{2,0,1:T(8,128)} %copy-done.11), calls=%async_computation.18 | async-start | bytes 8192 | tf_op jit(solution)/shard_map/jit(_roll_static)/slice | solution.py:99
  348.4 25.1 %copy-start.6 = (f32[8,4096]{1,0:T(8,128)}, f32[8,4096]{1,0:T(8,128)S(1)}, u32[]{:S(2)}) copy-start(f32[8,4096]{1,0:T(8,128)S(1)} %subtract_maximum_fusion.2) | copy-start | bytes 393220
  348.4 15.3 %all-to-all-start.9 = ((f32[8,32,128]{2,0,1:T(8,128)}), f32[8,32,128]{2,0,1:T(8,128)S(1)}, u32[]{:S(2)}, u32[]{:S(2)}) async-start(f32[8,32,128]{2,0,1:T(8,128)} %fusion.71), calls=%async_computation.9 | async-start | bytes 262144 | tf_op jit(solution)/shard_map/all_to_all | solution.py:126
  356.0 1.9 slice-start.6
  357.9 1.9 slice-start.8
  357.9 1.9 slice-start.9
  359.7 1.9 slice-start
  366.1 9.3 %copy-start.7 = (f32[8,4096]{1,0:T(8,128)}, f32[8,4096]{1,0:T(8,128)S(1)}, u32[]{:S(2)}) copy-start(f32[8,4096]{1,0:T(8,128)S(1)} %fusion.77) | copy-start | bytes 393220
  366.8 14.4 %all-to-all-start.10 = ((f32[8,32,128]{2,0,1:T(8,128)}), f32[8,32,128]{2,0,1:T(8,128)S(1)}, u32[]{:S(2)}, u32[]{:S(2)}) async-start(f32[8,32,128]{2,0,1:T(8,128)} %subtract_bitcast_fusion), calls=%async_computation.10 | async-start | bytes 262144 | tf_op jit(solution)/shard_map/all_to_all | solution.py:138
  385.8 15.5 %all-to-all-start.11 = ((f32[8,16,256]{2,0,1:T(8,128)}), f32[8,16,256]{2,0,1:T(8,128)S(1)}, u32[]{:S(2)}, u32[]{:S(2)}) async-start(f32[8,16,256]{2,0,1:T(8,128)} %bitcast.129), calls=%async_computation.11 | async-start | bytes 262144 | tf_op jit(solution)/shard_map/all_to_all | solution.py:149
  (11 other events, 20.2 us)
where the time goes:
time: 426 us; the launch traced here: 423 us
  blocking collectives  141 us (33%)
  matrix products  101 us (24%)
  starting transfers between devices  77.7 us (18%)
  waiting for transfers between devices  75.7 us (18%)
  other arithmetic  13.7 us (3%)
  between operations  5.45 us (1%)
  local copies, waits for them, and re-layouts  5 us (1%)
    psum x1, blocking collectives, body(): lax.psum((local_costs, local_targets), ('node', 'period'))  106 us
    dot_general x24, matrix products, pick_tiles(): jnp.einsum('ptn,tan->pta', values, table, precision=lax.Precision.HIGHEST)  53.8 us
    dot_general x24, matrix products, spread_tiles(): jnp.einsum('pta,tan->ptn', values, table, precision=lax.Precision.HIGHEST)  47 us
    all_to_all x2, waiting for transfers between devices, body(): lax.all_to_all(net, 'period', split_axis=1, concat_axis=0, tiled=True)  23.9 us
    all_to_all x2, waiting for transfers between devices, body(): lax.all_to_all(dual, 'period', split_axis=1, concat_axis=0, tiled=True)  21 us
    all_to_all x1, blocking collectives, body(): lax.all_to_all(stock, 'period', split_axis=0, concat_axis=1, tiled=True)  18.2 us
    all_to_all x1, blocking collectives, body(): lax.all_to_all(accumulated, 'period', split_axis=0, concat_axis=1, tiled=...  17.3 us
    all_to_all x1, starting transfers between devices, body(): lax.all_to_all(keep, 'period', split_axis=1, concat_axis=0, tiled=True)  15.8 us
  transfers between devices with their start and end apart: 11, of which 9 were waited for; matrix products, arithmetic and copies ran while one was open for 6% of the time, Pallas kernels for 0%

commit v1 on v0

v1 whole, which is shorter than its diff:
```python
import functools

import jax
import jax.numpy as jnp
from jax import lax
from jax.experimental import pallas as pl
from jax.experimental.pallas import tpu as pltpu
from jax.sharding import PartitionSpec as P

MESH = pl.DeviceIdType.MESH
ETA = 0.25
LANES = 128
ROWS = 8
PITCH = 16
PACK = 24
SENT = 18


def take(values, lanes):
    return jnp.take_along_axis(values, lanes, axis=1, mode="promise_in_bounds")


def sort_lanes(values):
    lane = lax.broadcasted_iota(jnp.int32, values.shape, 1)
    size = 2
    while size <= LANES:
        step = size // 2
        while step:
            other = take(values, lane ^ step)
            low = ((lane & size) == 0) == ((lane & step) == 0)
            values = jnp.where(low, jnp.minimum(values, other), jnp.maximum(values, other))
            step //= 2
        size *= 2
    return values


def kernel(sizes, *refs):
    nodes, periods, tiles, groups = sizes
    (
        prod_in, flow_in, cut_in, dual_in, cost_prod_in, cost_inner_in, cost_cut_in, target_in, keep_in,
        tail_in, head_in, cut_tail_in, cut_head_in,
        prod_out, flow_out, cut_out, dual_out,
        prod, flow, cut, dual, cost_prod, cost_inner, cost_cut, target, keep,
        tail, head, cut_tail, cut_head,
        kept, duals, targets, grown, price, price_late, net, change,
        keys, second, slot, ends_out, ends_in,
        pack, packs, flow_back, cost_back,
        swapped, swapped_late,
        send_a, recv_a, give_a, got_a,
        send_b, recv_b, give_b, got_b,
        send_c, recv_c, give_c, got_c,
        factor, square,
        in_sem, out_sem, send_sem, recv_sem,
    ) = refs
    me_node = lax.axis_index("node")
    me_period = lax.axis_index("period")
    horizon = periods * ROWS
    blocks = groups * tiles

    def tile(ref, number, pitch=ROWS):
        return ref[pl.ds(pl.multiple_of(number * pitch, ROWS), ROWS), :]

    def put(ref, number, values, pitch=ROWS):
        ref[pl.ds(pl.multiple_of(number * pitch, ROWS), ROWS), :] = values

    def lanes_of(ref, number):
        return jnp.broadcast_to(ref[pl.ds(number, 1), :], (ROWS, LANES))

    loads = [
        pltpu.make_async_copy(source, target_ref, in_sem.at[k])
        for k, (source, target_ref) in enumerate(
            (
                (keep_in, keep),
                (dual_in, dual),
                (cut_tail_in, cut_tail),
                (cut_head_in, cut_head),
                (cut_in, cut),
                (cost_cut_in, cost_cut),
                (tail_in, tail),
                (head_in, head),
                (target_in, target),
                (cost_prod_in, cost_prod),
                (cost_inner_in, cost_inner),
                (flow_in, flow),
                (prod_in, prod),
            )
        )
    ]
    for load in loads:
        load.start()

    barrier = pltpu.get_barrier_semaphore()

    def greet_period(k, _):
        pl.semaphore_signal(
            barrier, inc=1, device_id={"period": lax.rem(me_period + k, periods)}, device_id_type=MESH
        )
        return 0

    def greet_node(k, _):
        pl.semaphore_signal(
            barrier, inc=1, device_id={"node": lax.rem(me_node + k, nodes)}, device_id_type=MESH
        )
        return 0

    lax.fori_loop(1, periods, greet_period, 0)
    lax.fori_loop(1, nodes, greet_node, 0)

    def period_copy(source, target_ref, rows, phase, k):
        peer = lax.rem(me_period + k, periods)
        return pltpu.make_async_remote_copy(
            src_ref=source.at[pl.ds(pl.multiple_of(peer * ROWS, ROWS), rows), :],
            dst_ref=target_ref.at[pl.ds(pl.multiple_of(me_period * ROWS, ROWS), rows), :],
            send_sem=send_sem.at[phase],
            recv_sem=recv_sem.at[phase],
            device_id={"period": peer},
            device_id_type=MESH,
        )

    def node_copy(source, target_ref, pitch, rows, phase, k):
        peer = lax.rem(me_node + k, nodes)
        return pltpu.make_async_remote_copy(
            src_ref=source.at[pl.ds(pl.multiple_of(peer * pitch, ROWS), rows), :],
            dst_ref=target_ref.at[pl.ds(pl.multiple_of(me_node * pitch, ROWS), rows), :],
            send_sem=send_sem.at[phase],
            recv_sem=recv_sem.at[phase],
            device_id={"node": peer},
            device_id_type=MESH,
        )

    def spread_periods(source, target_ref, rows, phase):
        def one(k, _):
            period_copy(source, target_ref, rows, phase, k).start()
            return 0

        lax.fori_loop(1, periods, one, 0)
        put(target_ref, me_period, tile(source, me_period))

    def spread_nodes(source, target_ref, pitch, rows, phase):
        def one(k, _):
            node_copy(source, target_ref, pitch, rows, phase, k).start()
            return 0

        lax.fori_loop(1, nodes, one, 0)
        for part in range(pitch // ROWS):
            at = pl.ds(pl.multiple_of(me_node * pitch + part * ROWS, ROWS), ROWS)
            target_ref[at, :] = source[at, :]

    def await_rows(ref, rows, semaphore):
        whole = ref.at[pl.ds(0, rows), :]
        pltpu.make_async_copy(whole, whole, semaphore).wait()

    def arrived_periods(target_ref, rows, phase):
        await_rows(target_ref, (periods - 1) * rows, recv_sem.at[phase])

    def arrived_nodes(target_ref, rows, phase):
        await_rows(target_ref, (nodes - 1) * rows, recv_sem.at[phase])

    half = tiles // 2

    def put_summary(ref, row, values):
        ref[pl.ds(row, half, stride=ROWS), :] = values[:half]
        ref[pl.ds(row + 1, half, stride=ROWS), :] = values[half:]

    def get_summary(ref, row):
        return jnp.concatenate(
            [ref[pl.ds(row, half, stride=ROWS), :], ref[pl.ds(row + 1, half, stride=ROWS), :]], axis=0
        )

    def at_period(ref, t):
        return ref[pl.ds(t * tiles, tiles), :]

    row_number = lax.broadcasted_iota(jnp.int32, (ROWS, LANES), 0)
    none = jnp.zeros((ROWS, LANES), jnp.float32)

    loads[0].wait()
    loads[1].wait()
    product = None
    square_sum = None
    for t in range(ROWS):
        share = keep[pl.ds(t, tiles, stride=ROWS), :]
        kept[pl.ds(t * tiles, tiles), :] = share
        product = share if product is None else product * share
        grown[pl.ds(t * tiles, tiles), :] = product
        square_sum = product * product if square_sum is None else square_sum + product * product
    passed = None
    for t in reversed(range(ROWS)):
        value = dual[pl.ds(t, tiles, stride=ROWS), :]
        duals[pl.ds(t * tiles, tiles), :] = value
        passed = value if passed is None else value + passed
        passed = passed * at_period(kept, t)
    put_summary(send_a, 0, product)
    put_summary(send_a, 2, passed)
    put_summary(send_a, 4, square_sum)

    for k in (2, 3, 4, 5):
        loads[k].wait()

    def pack_one(d, _):
        put(pack, d, tile(cut, d), PACK)
        pack[pl.ds(pl.multiple_of(d * PACK + ROWS, ROWS), ROWS), :] = tile(cost_cut, d)
        return 0

    lax.fori_loop(0, nodes, pack_one, 0)
    cut_tail[...] = cut_tail[...] & (LANES - 1)
    cut_head[...] = cut_head[...] & (LANES - 1)
    pack[pl.ds(2 * ROWS, nodes, stride=PACK), :] = cut_tail[...].astype(jnp.float32)
    pack[pl.ds(2 * ROWS + 1, nodes, stride=PACK), :] = cut_head[...].astype(jnp.float32)

    pl.semaphore_wait(barrier, periods + nodes - 2)
    spread_periods(send_a, recv_a, 6, 0)
    spread_nodes(pack, packs, PACK, SENT, 6)

    for k in (8, 9, 10):
        loads[k].wait()

    def square_one(t, sums):
        costs, wanted = sums
        value = tile(target, t)
        wanted = wanted + value * value
        value = tile(cost_prod, t)
        costs = costs + value * value
        value = tile(cost_cut, t)
        costs = costs + value * value
        for group in range(groups):
            value = tile(cost_inner, group * tiles + t)
            costs = costs + value * value
        return costs, wanted

    costs, wanted = lax.fori_loop(0, tiles, square_one, (none, none))
    costs = jnp.sum(costs, axis=0, keepdims=True)
    wanted = jnp.sum(wanted, axis=0, keepdims=True)

    arrived_periods(recv_a, 6, 0)
    entering = none
    for j in reversed(range(periods)):
        block = tile(recv_a, j)
        ratio = jnp.where(row_number < 2, block, pltpu.roll(block, 2, 0))
        put(factor, j, ratio)
        put(square, j, pltpu.roll(block, ROWS - 2, 0))
        put(give_a, j, jnp.where(row_number < 1, costs, jnp.where(row_number < 2, wanted, entering)))
        entering = block + ratio * entering
    spread_periods(give_a, got_a, 4, 1)

    loads[6].wait()
    loads[7].wait()
    tail[...] = tail[...] & (LANES - 1)
    head[...] = head[...] & (LANES - 1)

    def keyed(first, other):
        lane = lax.broadcasted_iota(jnp.int32, first.shape, 1)
        return (first * (LANES * LANES) + other * LANES + lane).astype(jnp.float32)

    keys[pl.ds(0, blocks), :] = keyed(tail[...], head[...])
    keys[pl.ds(blocks, blocks), :] = keyed(head[...], tail[...])
    keys[pl.ds(2 * blocks, nodes), :] = keyed(cut_tail[...], cut_head[...])
    keys[pl.ds(2 * blocks + nodes, nodes), :] = keyed(cut_head[...], cut_tail[...])
    batch = 128

    def sort_batch(k, _):
        at = pl.ds(pl.multiple_of(k * batch, batch), batch)
        ordered = sort_lanes(keys[at, :]).astype(jnp.int32)
        second[at, :] = lax.shift_right_logical(ordered, 7) & (LANES - 1)
        slot[at, :] = ordered & (LANES - 1)
        return 0

    lax.fori_loop(0, (2 * blocks + 2 * nodes) // batch, sort_batch, 0)

    loads[11].wait()
    loads[12].wait()

    def reorder(t, _):
        for group in range(groups):
            j = group * tiles + t
            lanes = lanes_of(slot, j)
            put(flow, j, take(tile(flow, j), lanes))
            put(cost_inner, j, take(tile(cost_inner, j), lanes))
        lanes = lanes_of(slot, 2 * blocks + t)
        put(cut, t, take(tile(cut, t), lanes))
        put(cost_cut, t, take(tile(cost_cut, t), lanes))
        return 0

    lax.fori_loop(0, tiles, reorder, 0)

    for t in range(ROWS):
        targets[pl.ds(t * tiles, tiles), :] = target[pl.ds(t, tiles, stride=ROWS), :]

    arrived_periods(got_a, 4, 1)
    entering = get_summary(got_a, 2)
    for t in reversed(range(ROWS)):
        entering = at_period(duals, t) + entering
        price[pl.ds(t, tiles, stride=PITCH), :] = entering * (1.0 / horizon)
        entering = entering * at_period(kept, t)
    for row in range(2):
        column = jnp.sum(got_a[pl.ds(row, periods, stride=ROWS), :], axis=0, keepdims=True)
        price[pl.ds(ROWS + row, tiles, stride=PITCH), :] = jnp.broadcast_to(column, (tiles, LANES))
    spread_nodes(price, swapped, PITCH, ROWS + 2, 7)

    arrived_nodes(packs, SENT, 6)
    ends_out[...] = take(
        packs[pl.ds(2 * ROWS + 1, nodes, stride=PACK), :], slot[pl.ds(2 * blocks, nodes), :]
    ).astype(jnp.int32)
    ends_in[...] = take(
        packs[pl.ds(2 * ROWS, nodes, stride=PACK), :], slot[pl.ds(2 * blocks + nodes, nodes), :]
    ).astype(jnp.int32)

    def reorder_back(d, _):
        lanes = lanes_of(slot, 2 * blocks + nodes + d)
        put(flow_back, d, take(tile(packs, d, PACK), lanes))
        at = pl.ds(pl.multiple_of(d * PACK + ROWS, ROWS), ROWS)
        put(cost_back, d, take(packs[at, :], lanes))
        return 0

    lax.fori_loop(0, nodes, reorder_back, 0)

    def update_inner(prices, tau):
        def one(t, _):
            here = tile(prices, t, PITCH)
            old = tile(prod, t)
            new = jnp.maximum(old - tau * (tile(cost_prod, t) - here), 0.0)
            put(prod, t, new)
            total = 2.0 * new - old
            for group in range(groups):
                j = group * tiles + t
                there = take(tile(prices, lax.rem(t + group, tiles), PITCH), lanes_of(second, j))
                old = tile(flow, j)
                new = jnp.maximum(old - tau * (tile(cost_inner, j) - (there - here)), 0.0)
                put(flow, j, new)
                moved = 2.0 * new - old
                put(change, j, moved)
                total = total - moved
            put(net, t, total)
            return 0

        lax.fori_loop(0, tiles, one, 0)

    def update_cut(prices, others, tau):
        def one(t, _):
            here = tile(prices, t, PITCH)
            other = tile(others, t, PITCH)
            total = tile(net, t)
            there = take(other, lanes_of(ends_out, t))
            old = tile(cut, t)
            new = jnp.maximum(old - tau * (tile(cost_cut, t) - (there - here)), 0.0)
            put(cut, t, new)
            total = total - (2.0 * new - old)
            there = take(other, lanes_of(ends_in, t))
            old = tile(flow_back, t)
            new = jnp.maximum(old - tau * (tile(cost_back, t) - (here - there)), 0.0)
            put(flow_back, t, new)
            total = total + (2.0 * new - old)
            for group in range(groups):
                j = group * tiles + lax.rem(t - group + tiles, tiles)
                total = total + take(tile(change, j), lanes_of(second, blocks + j))
            put(net, t, total)
            return 0

        lax.fori_loop(0, tiles, one, 0)

    arrived_nodes(swapped, ROWS + 2, 7)
    sums = [
        jnp.sum(swapped[pl.ds(ROWS + row, nodes, stride=PITCH), :], keepdims=True) for row in range(2)
    ]
    omega = jnp.sqrt(sums[0] / sums[1])
    tau = jnp.broadcast_to(ETA / omega, (ROWS, LANES))
    sigma = ETA * omega
    sigma_tile = jnp.broadcast_to(sigma, (ROWS, LANES)) * (1.0 / horizon)
    sigma_wide = jnp.broadcast_to(sigma, (tiles, LANES))
    update_inner(price, tau)
    update_cut(price, swapped, tau)

    stock = None
    for t in range(ROWS):
        value = net[pl.ds(t, tiles, stride=ROWS), :]
        stock = value if stock is None else at_period(kept, t) * stock + value
        duals[pl.ds(t * tiles, tiles), :] = at_period(duals, t) + sigma_wide * (
            at_period(targets, t) - stock * (1.0 / horizon)
        )
    passed = None
    for t in reversed(range(ROWS)):
        value = at_period(duals, t)
        passed = value if passed is None else value + passed
        passed = passed * at_period(kept, t)
    put_summary(send_b, 0, stock)
    put_summary(send_b, 2, passed)
    spread_periods(send_b, recv_b, 4, 2)
    arrived_periods(recv_b, 4, 2)
    parts = [tile(recv_b, j) for j in range(periods)]
    entering = none
    entered = []
    for j in range(periods):
        entered.append(entering)
        entering = parts[j] + tile(factor, j) * entering
    entering = none
    for j in reversed(range(periods)):
        put(give_b, j, jnp.where(row_number < 2, entered[j], entering))
        answer = parts[j] - sigma_tile * tile(square, j) * pltpu.roll(entered[j], 2, 0)
        entering = answer + tile(factor, j) * entering
    spread_periods(give_b, got_b, 4, 3)
    arrived_periods(got_b, 4, 3)
    stock = get_summary(got_b, 0) * (sigma_wide * (1.0 / horizon))
    entering = get_summary(got_b, 2)
    for t in reversed(range(ROWS)):
        value = at_period(duals, t) - at_period(grown, t) * stock
        duals[pl.ds(t * tiles, tiles), :] = value
        entering = value + entering
        price_late[pl.ds(t, tiles, stride=PITCH), :] = entering * (1.0 / horizon)
        entering = entering * at_period(kept, t)

    spread_nodes(price_late, swapped_late, PITCH, ROWS, 8)
    update_inner(price_late, tau)
    arrived_nodes(swapped_late, ROWS, 8)
    update_cut(price_late, swapped_late, tau)
    stock = None
    for t in range(ROWS):
        value = net[pl.ds(t, tiles, stride=ROWS), :]
        stock = value if stock is None else at_period(kept, t) * stock + value
        duals[pl.ds(t * tiles, tiles), :] = at_period(duals, t) + sigma_wide * (
            at_period(targets, t) - stock * (1.0 / horizon)
        )
    put_summary(send_c, 0, stock)
    spread_periods(send_c, recv_c, 2, 4)
    store_prod = pltpu.make_async_copy(prod, prod_out, out_sem.at[0])
    store_prod.start()
    arrived_periods(recv_c, 2, 4)
    entering = none
    for j in range(periods):
        put(give_c, j, entering)
        entering = tile(recv_c, j) + tile(factor, j) * entering
    spread_periods(give_c, got_c, 2, 5)

    def restore(t, _):
        for group in range(groups):
            j = group * tiles + t
            put(flow, j, take(tile(flow, j), lanes_of(tail, j)))
        put(cut, t, take(tile(cut, t), lanes_of(cut_tail, t)))
        return 0

    lax.fori_loop(0, tiles, restore, 0)
    store_flow = pltpu.make_async_copy(flow, flow_out, out_sem.at[1])
    store_flow.start()
    store_cut = pltpu.make_async_copy(cut, cut_out, out_sem.at[2])
    store_cut.start()

    arrived_periods(got_c, 2, 5)
    stock = get_summary(got_c, 0) * (sigma_wide * (1.0 / horizon))
    for t in range(ROWS):
        dual[pl.ds(t, tiles, stride=ROWS), :] = at_period(duals, t) - at_period(grown, t) * stock
    store_dual = pltpu.make_async_copy(dual, dual_out, out_sem.at[3])
    store_dual.start()

    for phase, (ref, rows) in enumerate(
        ((send_a, 6), (give_a, 4), (send_b, 4), (give_b, 4), (send_c, 2), (give_c, 2))
    ):
        await_rows(ref, (periods - 1) * rows, send_sem.at[phase])
    for phase, ref, rows in ((6, pack, SENT), (7, price, ROWS + 2), (8, price_late, ROWS)):
        await_rows(ref, (nodes - 1) * rows, send_sem.at[phase])
    for store in (store_prod, store_flow, store_cut, store_dual):
        store.wait()


def solution(mesh):
    nodes, periods = mesh.shape["node"], mesh.shape["period"]

    def to_tiles(values):
        rows, columns = values.shape
        return values.reshape(rows, columns // LANES, LANES).transpose(1, 0, 2).reshape(-1, LANES)

    def from_tiles(values):
        count = values.shape[0] // ROWS
        return values.reshape(count, ROWS, LANES).transpose(1, 0, 2).reshape(ROWS, count * LANES)

    def body(*operands):
        floats = [to_tiles(values) for values in operands[:9]]
        indices = [values.reshape(-1, LANES) for values in operands[9:]]
        tiles = floats[0].shape[0] // ROWS
        groups = floats[1].shape[0] // floats[0].shape[0]
        blocks = tiles * groups
        slab = (tiles * ROWS, LANES)
        arcs = (blocks * ROWS, LANES)
        ring = (periods * ROWS, LANES)

        def room(shape, kind=jnp.float32):
            return pltpu.VMEM(shape, kind)

        scratch = [
            room(slab), room(arcs), room(slab), room(slab), room(slab), room(arcs), room(slab), room(slab), room(slab),
            room((blocks, LANES), jnp.int32), room((blocks, LANES), jnp.int32),
            room((tiles, LANES), jnp.int32), room((tiles, LANES), jnp.int32),
            room(slab), room(slab), room(slab), room(slab),
            room((tiles * PITCH, LANES)), room((tiles * PITCH, LANES)), room(slab), room(arcs),
            room((2 * blocks + 2 * nodes, LANES)),
            room((2 * blocks + 2 * nodes, LANES), jnp.int32), room((2 * blocks + 2 * nodes, LANES), jnp.int32),
            room((nodes, LANES), jnp.int32), room((nodes, LANES), jnp.int32),
            room((nodes * PACK, LANES)), room((nodes * PACK, LANES)), room(slab), room(slab),
            room((nodes * PITCH, LANES)), room((nodes * PITCH, LANES)),
        ] + [room(ring)] * 14 + [
            pltpu.SemaphoreType.DMA((13,)),
            pltpu.SemaphoreType.DMA((4,)),
            pltpu.SemaphoreType.DMA((9,)),
            pltpu.SemaphoreType.DMA((9,)),
        ]
        anywhere = pl.BlockSpec(memory_space=pl.ANY)
        outputs = pl.pallas_call(
            functools.partial(kernel, (nodes, periods, tiles, groups)),
            out_shape=[jax.ShapeDtypeStruct(shape, jnp.float32) for shape in (slab, arcs, slab, slab)],
            in_specs=[anywhere] * 13,
            out_specs=[anywhere] * 4,
            scratch_shapes=scratch,
            compiler_params=pltpu.CompilerParams(
                collective_id=0, has_side_effects=True, vmem_limit_bytes=32 * 1024 * 1024
            ),
        )(*floats, *indices)
        return tuple(from_tiles(values) for values in outputs)

    both, node = P("period", "node"), P("node")
    return jax.shard_map(
        body,
        mesh=mesh,
        in_specs=(both,) * 9 + (node,) * 4,
        out_specs=(both,) * 4,
        check_vma=False,
    )
```

time: 426 us -> 97.2 us (0.23)
  blocking collectives: 141 us -> 0 us
  matrix products: 101 us -> 0 us
  Pallas kernels: 0 us -> 81.5 us
  starting transfers between devices: 77.7 us -> 0 us
  waiting for transfers between devices: 75.7 us -> 0 us
  other arithmetic: 13.7 us -> 0 us
  local copies, waits for them, and re-layouts: 5 us -> 14.5 us
  between operations: 5.45 us -> 0.67 us
    psum x1 -> x0, blocking collectives: 106 us -> none  [body(): lax.psum((local_costs, local_targets), ('node', 'period'))]
    dot_general x48 -> x0, matrix products: 101 us -> none  [the longest x24 53.8 us: pick_tiles(): jnp.einsum('ptn,tan->pta', values, table, precision=lax.Precision.HIGHEST)]
    pallas_call x0 -> x1, Pallas kernels: none -> 81.5 us  [body(): pl.pallas_call(functools.partial(kernel, (nodes, periods, tiles, groups))...]
    all_to_all x11 -> x0, starting transfers between devices: 77.7 us -> none  [the longest x1 15.8 us: body(): lax.all_to_all(keep, 'period', split_axis=1, concat_axis=0, tiled=True)]
    all_to_all x11 -> x0, waiting for transfers between devices: 75.7 us -> none  [the longest x2 23.9 us: body(): lax.all_to_all(net, 'period', split_axis=1, concat_axis=0, tiled=True)]
    all_to_all x2 -> x0, blocking collectives: 35.4 us -> none  [the longest x1 18.2 us: body(): lax.all_to_all(stock, 'period', split_axis=0, concat_axis=1, tiled=True)]
    unnamed x98 -> x30, local copies, waits for them, and re-layouts: 0.38 us -> 14.5 us
    reduce_sum x4 -> x0, other arithmetic: 5.67 us -> none  [the longest x1 1.86 us: body(): jnp.sum(cost_inner * cost_inner)]
  transfers between devices with their start and end apart: 11 -> 0, of which waited for: 9 -> 0; matrix products, arithmetic and copies ran while one was open for 6% -> 0% of each run, Pallas kernels for 0% -> 0%
where the time goes in v1:
time: 97.2 us; the launch traced here: 96.7 us
  Pallas kernels  81.5 us (84%)
  local copies, waits for them, and re-layouts  14.5 us (15%)
    pallas_call x1, Pallas kernels, body(): pl.pallas_call(functools.partial(kernel, (nodes, periods, tiles, groups))...  81.5 us
    unnamed x30, local copies, waits for them, and re-layouts  14.5 us

profile of v1, /device:TPU:1, one launch (start us, length us, event | category | flops | bytes accessed | tf_op | source)
XLA Modules:
  0.0 96.7 jit_solution(1119614010391352378)
XLA Ops:
  0.6 0.0 copy-start.11
  0.6 0.7 copy-done.11
  1.4 0.0 copy-start
  1.4 1.1 %copy-done = f32[8,20480]{1,0:T(8,128)S(1)} copy-done((f32[8,20480]{1,0:T(8,128)S(1)}, f32[8,20480]{1,0:T(8,128)}, u32[]{:S(2)}) %copy-start) | copy-done | bytes 655384
  2.4 0.0 copy-start.1
  2.4 1.1 %copy-done.1 = f32[8,20480]{1,0:T(8,128)S(1)} copy-done((f32[8,20480]{1,0:T(8,128)S(1)}, f32[8,20480]{1,0:T(8,128)}, u32[]{:S(2)}) %copy-start.1) | copy-done | bytes 655384
  3.5 0.0 copy-start.2
  3.5 0.9 copy-done.2
  4.4 0.0 copy-start.3
  4.4 0.9 copy-done.3
  5.3 0.0 copy-start.4
  5.3 0.9 copy-done.4
  6.2 0.0 copy-start.5
  6.2 0.9 copy-done.5
  7.1 0.0 copy-start.6
  7.2 0.9 copy-done.6
  8.1 0.0 copy-start.7
  8.1 0.9 copy-done.7
  9.0 0.0 copy-start.8
  9.0 0.9 copy-done.8
  9.9 0.0 copy-start.9
  9.9 0.9 copy-done.9
  10.8 0.0 copy-start.10
  10.8 0.9 copy-done.10
  11.6 0.0 copy-start.12
  11.6 0.7 copy-done.12
  12.4 81.5 %shard_map.156 = (f32[256,128]{1,0:T(8,128)S(1)}, f32[1280,128]{1,0:T(8,128)S(1)}, f32[256,128]{1,0:T(8,128)S(1)}, f32[256,128]{1,0:T(8,128)S(1)}) custom-call(f32[256,128]{1,0:T(8,128)S(1)} %bitcast.72, f32[1280,128]{1,0:T(8,128)S(1)} %bitcast.70, f32[256,128]{1,0:T(8,128)S(1)} %bitcast.73, f32[256,128]{1,0:T(8,128)S(1)} %bitcast.74, ...), custom_call_target="tpu_custom_call" | custom-call | tf_op jit(solution)/shard_map/pallas_call | solution.py:504
  93.9 0.7 copy.21
  94.6 0.8 copy.22
  95.4 0.7 copy.23
  96.0 0.7 copy.24
Async XLA Ops:
  0.6 0.7 copy-start.11
  1.4 1.1 %copy-start = (f32[8,20480]{1,0:T(8,128)S(1)}, f32[8,20480]{1,0:T(8,128)}, u32[]{:S(2)}) copy-start(f32[8,20480]{1,0:T(8,128)} %param.14) | copy-start | bytes 1966084
  2.4 1.1 %copy-start.1 = (f32[8,20480]{1,0:T(8,128)S(1)}, f32[8,20480]{1,0:T(8,128)}, u32[]{:S(2)}) copy-start(f32[8,20480]{1,0:T(8,128)} %param.18) | copy-start | bytes 1966084
  3.5 0.9 copy-start.2
  4.4 0.9 copy-start.3
  5.3 0.9 copy-start.4
  6.2 0.9 copy-start.5
  7.1 0.9 copy-start.6
  8.1 0.9 copy-start.7
  9.0 0.9 copy-start.8
  9.9 0.9 copy-start.9
  10.8 0.9 copy-start.10
  11.6 0.7 copy-start.12

commit v2 on v1

v2 whole, which is shorter than its diff:
```python
import functools

import jax
import jax.numpy as jnp
from jax import lax
from jax.experimental import pallas as pl
from jax.experimental.pallas import tpu as pltpu
from jax.sharding import PartitionSpec as P

MESH = pl.DeviceIdType.MESH
ETA = 0.25
LANES = 128
ROWS = 8
PACK = 40
SENT = 34
UNROLL = 4
LIMIT = 56 * 1024 * 1024


def take(values, lanes):
    return jnp.take_along_axis(values, lanes, axis=1, mode="promise_in_bounds")


def sort_lanes(values):
    lane = lax.broadcasted_iota(jnp.int32, values.shape, 1)
    size = 2
    while size <= LANES:
        step = size // 2
        while step:
            other = take(values, lane ^ step)
            low = ((lane & size) == 0) == ((lane & step) == 0)
            values = jnp.where(low, jnp.minimum(values, other), jnp.maximum(values, other))
            step //= 2
        size *= 2
    return values


def kernel(sizes, *refs):
    nodes, periods, tiles, groups = sizes
    (
        prod_in, flow_in, cut_in, dual_in, cost_prod_in, cost_inner_in, cost_cut_in, target_in, keep_in,
        tail_in, head_in, cut_tail_in, cut_head_in,
        prod, flow, cut, dual,
        cost_prod, cost_inner, cost_cut, target, keep,
        tail, head, cut_tail, cut_head,
        kept, duals, targets, grown, kept_far, grown_far,
        price, price_far, net, change,
        keys, second, slot, ends_out, ends_in,
        pack, packs, flow_back, cost_back,
        late, lates, part, parts,
        send_a, recv_a, give_a, got_a, far_a, send_s, recv_s,
        send_b, recv_b, give_b, got_b, far_b,
        send_c, recv_c, give_c, got_c,
        factor, factor_c,
        in_sem, send_sem, recv_sem,
    ) = refs
    me_node = lax.axis_index("node")
    me_period = lax.axis_index("period")
    horizon = periods * ROWS
    blocks = groups * tiles
    chunks = periods // 2
    reach = chunks // 2
    ranks = tiles // chunks
    me_chunk = lax.rem(me_period, chunks)

    def rows_at(number, rows=ROWS, pitch=ROWS):
        return pl.ds(pl.multiple_of(number * pitch, ROWS), rows)

    def tile(ref, number):
        return ref[rows_at(number), :]

    def put(ref, number, values):
        ref[rows_at(number), :] = values

    def lanes_of(ref, number):
        return jnp.broadcast_to(ref[pl.ds(number, 1), :], (ROWS, LANES))

    loads = [
        pltpu.make_async_copy(source, target_ref, in_sem.at[k])
        for k, (source, target_ref) in enumerate(
            (
                (keep_in, keep),
                (dual_in, dual),
                (cut_tail_in, cut_tail),
                (cut_head_in, cut_head),
                (cut_in, cut),
                (cost_cut_in, cost_cut),
                (tail_in, tail),
                (head_in, head),
                (target_in, target),
                (cost_prod_in, cost_prod),
                (cost_inner_in, cost_inner),
                (flow_in, flow),
                (prod_in, prod),
            )
        )
    ]
    for load in loads:
        load.start()

    def greet(device):
        pl.semaphore_signal(
            pltpu.get_barrier_semaphore(), inc=1, device_id=device, device_id_type=MESH
        )

    def greet_period(k, _):
        greet({"period": lax.rem(me_period + k, periods)})
        return 0

    def greet_node(k, _):
        greet({"node": lax.rem(me_node + k, nodes)})
        return 0

    node_chunk = lax.rem(me_node, chunks)
    source_plane = node_chunk + chunks * (
        lax.rem(me_period + periods + reach - node_chunk, periods) // chunks
    )

    def greet_far(k, _):
        greet({"node": lax.rem(me_node + k, nodes), "period": source_plane})
        return 0

    lax.fori_loop(1, periods, greet_period, 0)
    lax.fori_loop(1, nodes, greet_node, 0)
    lax.fori_loop(1, nodes, greet_far, 0)
    far_count = jnp.where(me_chunk == node_chunk, ranks - 1, ranks) * chunks

    def start(source, target_ref, source_rows, target_rows, phase, device):
        pltpu.make_async_remote_copy(
            src_ref=source.at[source_rows, :],
            dst_ref=target_ref.at[target_rows, :],
            send_sem=send_sem.at[phase],
            recv_sem=recv_sem.at[phase],
            device_id=device,
            device_id_type=MESH,
        ).start()

    def spread_owners(source, target_ref, rows, phase):
        def one(k, _):
            peer = lax.rem(me_period + k, periods)
            start(
                source, target_ref, rows_at(lax.rem(peer, chunks), rows), rows_at(me_period, rows), phase,
                {"period": peer},
            )
            return 0

        lax.fori_loop(1, periods, one, 0)
        put(target_ref, me_period, tile(source, me_chunk))

    def served(i):
        return lax.rem(me_period + periods - reach + i, periods)

    def give_back(source, target_ref, rows, phase):
        def one(i, _):
            @pl.when(i != reach)
            def _():
                peer = served(i)
                start(
                    source, target_ref, rows_at(peer, rows), rows_at(me_chunk, rows), phase,
                    {"period": peer},
                )

            return 0

        lax.fori_loop(0, chunks, one, 0)
        put(target_ref, me_chunk, tile(source, me_period))

    def give_far(source, target_ref, phase):
        for rank in range(ranks):
            to = me_chunk + rank * chunks

            @pl.when(to != me_node)
            def _():
                def one(i, _):
                    peer = served(i)
                    start(
                        source, target_ref,
                        pl.ds(pl.multiple_of(peer * ROWS, ROWS) + 2 * rank, 2), rows_at(me_node, 2), phase,
                        {"node": to, "period": peer},
                    )
                    return 0

                lax.fori_loop(0, chunks, one, 0)

    def spread_nodes(source, target_ref, pitch, rows, phase, same=False):
        def one(k, _):
            peer = lax.rem(me_node + k, nodes)
            start(
                source, target_ref, rows_at(0 if same else peer, rows, pitch), rows_at(me_node, rows, pitch), phase,
                {"node": peer},
            )
            return 0

        lax.fori_loop(1, nodes, one, 0)

    def await_rows(ref, rows, semaphore):
        whole = ref.at[pl.ds(0, rows), :]
        pltpu.make_async_copy(whole, whole, semaphore).wait()

    def put_summary(ref, row, values, pitch=2):
        for rank in range(ranks):
            ref[pl.ds(pitch * rank + row, chunks, stride=ROWS), :] = values[
                rank * chunks : (rank + 1) * chunks
            ]

    def get_summary(ref, row, pitch=2):
        return jnp.concatenate(
            [ref[pl.ds(pitch * rank + row, chunks, stride=ROWS), :] for rank in range(ranks)], axis=0
        )

    def at_period(ref, t):
        return ref[pl.ds(t * tiles, tiles), :]

    def by_node(ref, t, pitch=ROWS):
        return ref[pl.ds(t, tiles, stride=pitch), :]

    def chain_back(values, shares, entering, target_ref):
        for t in reversed(range(ROWS)):
            entering = values(t) + entering
            target_ref[pl.ds(t, tiles, stride=ROWS), :] = entering * (1.0 / horizon)
            entering = entering * at_period(shares, t)

    def passed_back():
        passed = None
        for t in reversed(range(ROWS)):
            value = at_period(duals, t)
            passed = value if passed is None else value + passed
            passed = passed * at_period(kept, t)
        return passed

    def products(share_of, shares, target_ref):
        product = None
        square_sum = None
        for t in range(ROWS):
            share = share_of(t)
            shares[pl.ds(t * tiles, tiles), :] = share
            product = share if product is None else product * share
            target_ref[pl.ds(t * tiles, tiles), :] = product
            square = product * product
            square_sum = square if square_sum is None else square_sum + square
        return product, square_sum

    even = (lax.broadcasted_iota(jnp.int32, (ROWS, LANES), 0) & 1) == 0
    none = jnp.zeros((ROWS, LANES), jnp.float32)

    loads[0].wait()
    loads[1].wait()
    product, square_sum = products(lambda t: by_node(keep, t), kept, grown)
    for t in range(ROWS):
        duals[pl.ds(t * tiles, tiles), :] = by_node(dual, t)
    put_summary(send_a, 0, product)
    put_summary(send_a, 1, passed_back())
    put_summary(send_s, 1, square_sum)

    for k in (2, 3, 4, 5):
        loads[k].wait()

    def pack_one(step, _):
        for k in range(UNROLL):
            d = step * UNROLL + k
            for place, ref in enumerate((cut, cost_cut, keep, dual)):
                pack[rows_at(d * (PACK // ROWS) + place), :] = tile(ref, d)
        return 0

    lax.fori_loop(0, nodes // UNROLL, pack_one, 0)
    cut_tail[...] = cut_tail[...] & (LANES - 1)
    cut_head[...] = cut_head[...] & (LANES - 1)
    pack[pl.ds(4 * ROWS, nodes, stride=PACK), :] = cut_tail[...].astype(jnp.float32)
    pack[pl.ds(4 * ROWS + 1, nodes, stride=PACK), :] = cut_head[...].astype(jnp.float32)

    for k in (8, 9, 10):
        loads[k].wait()

    def square_one(t, sums):
        costs, wanted = sums
        value = tile(target, t)
        wanted = wanted + value * value
        value = tile(cost_prod, t)
        first = value * value
        value = tile(cost_cut, t)
        other = value * value
        for group in range(groups):
            value = tile(cost_inner, group * tiles + t)
            if group % 2:
                first = first + value * value
            else:
                other = other + value * value
        return costs + (first + other), wanted

    costs, wanted = lax.fori_loop(0, tiles, square_one, (none, none))
    put_summary(send_s, 0, jnp.zeros((tiles, LANES), jnp.float32))
    for row, value in ((0, costs), (2, wanted)):
        value = jnp.sum(value, axis=0, keepdims=True)
        send_s[pl.ds(row, chunks, stride=ROWS), :] = jnp.broadcast_to(value, (chunks, LANES))

    loads[6].wait()
    loads[7].wait()
    tail[...] = tail[...] & (LANES - 1)
    head[...] = head[...] & (LANES - 1)

    def keyed(first, other):
        lane = lax.broadcasted_iota(jnp.int32, first.shape, 1)
        return (first * (LANES * LANES) + other * LANES + lane).astype(jnp.float32)

    keys[pl.ds(0, blocks), :] = keyed(tail[...], head[...])
    keys[pl.ds(blocks, blocks), :] = keyed(head[...], tail[...])
    keys[pl.ds(2 * blocks, nodes), :] = keyed(cut_tail[...], cut_head[...])
    keys[pl.ds(2 * blocks + nodes, nodes), :] = keyed(cut_head[...], cut_tail[...])
    batch = 128

    def sort_batch(k, _):
        at = pl.ds(pl.multiple_of(k * batch, batch), batch)
        ordered = sort_lanes(keys[at, :]).astype(jnp.int32)
        second[at, :] = lax.shift_right_logical(ordered, 7) & (LANES - 1)
        slot[at, :] = ordered & (LANES - 1)
        return 0

    lax.fori_loop(0, (2 * blocks + 2 * nodes) // batch, sort_batch, 0)

    pl.semaphore_wait(pltpu.get_barrier_semaphore(), periods + nodes - 2 + far_count)
    spread_owners(send_a, recv_a, ROWS, 0)
    spread_owners(send_s, recv_s, ROWS, 1)
    spread_nodes(pack, packs, PACK, SENT, 2)

    loads[11].wait()
    loads[12].wait()

    def reorder(step, _):
        moved = []
        for k in range(UNROLL):
            t = step * UNROLL + k
            for group in range(groups):
                j = group * tiles + t
                lanes = lanes_of(slot, j)
                moved.append((flow, j, take(tile(flow, j), lanes)))
                moved.append((cost_inner, j, take(tile(cost_inner, j), lanes)))
            lanes = lanes_of(slot, 2 * blocks + t)
            moved.append((cut, t, take(tile(cut, t), lanes)))
            moved.append((cost_cut, t, take(tile(cost_cut, t), lanes)))
        for ref, number, values in moved:
            put(ref, number, values)
        return 0

    lax.fori_loop(0, tiles // UNROLL, reorder, 0)
    for t in range(ROWS):
        targets[pl.ds(t * tiles, tiles), :] = by_node(target, t)

    await_rows(recv_a, (periods - 1) * ROWS, recv_sem.at[0])
    entering = none
    for j in reversed(range(periods)):
        block = tile(recv_a, j)
        ratio = jnp.where(even, block, pltpu.roll(block, 1, 0))
        put(factor, j, ratio)
        put(give_a, j, entering)
        entering = block + ratio * entering
    give_back(give_a, got_a, ROWS, 3)
    give_far(give_a, far_a, 4)

    await_rows(recv_s, (periods - 1) * ROWS, recv_sem.at[1])
    total = none
    for j in range(periods):
        total = total + tile(recv_s, j)
        factor_c[pl.ds(j * ROWS, ranks), :] = factor[pl.ds(j * ROWS, ranks, stride=2), :]
    part[...] = total
    spread_nodes(part, parts, ROWS, 4, 5, same=True)
    put(parts, me_node, total)

    await_rows(packs, (nodes - 1) * SENT, recv_sem.at[2])
    packs[rows_at(me_node, PACK, PACK), :] = pack[rows_at(me_node, PACK, PACK), :]
    ends_out[...] = take(
        packs[pl.ds(4 * ROWS + 1, nodes, stride=PACK), :], slot[pl.ds(2 * blocks, nodes), :]
    ).astype(jnp.int32)
    ends_in[...] = take(
        packs[pl.ds(4 * ROWS, nodes, stride=PACK), :], slot[pl.ds(2 * blocks + nodes, nodes), :]
    ).astype(jnp.int32)

    def reorder_back(step, _):
        moved = []
        for k in range(UNROLL):
            d = step * UNROLL + k
            lanes = lanes_of(slot, 2 * blocks + nodes + d)
            for place, ref in enumerate((flow_back, cost_back)):
                moved.append((ref, d, take(tile(packs, d * (PACK // ROWS) + place), lanes)))
        for ref, number, values in moved:
            put(ref, number, values)
        return 0

    lax.fori_loop(0, nodes // UNROLL, reorder_back, 0)
    products(lambda t: packs[pl.ds(2 * ROWS + t, nodes, stride=PACK), :], kept_far, grown_far)

    def update_inner(tau):
        def one(step, _):
            stores = []
            for k in range(UNROLL):
                t = step * UNROLL + k
                here = tile(price, t)
                old = tile(prod, t)
                new = jnp.maximum(old - tau * (tile(cost_prod, t) - here), 0.0)
                stores.append((prod, t, new))
                total = 2.0 * new - old
                for group in range(groups):
                    j = group * tiles + t
                    there = take(tile(price, lax.rem(t + group, tiles)), lanes_of(second, j))
                    old = tile(flow, j)
                    new = jnp.maximum(old - tau * (tile(cost_inner, j) - (there - here)), 0.0)
                    moved = 2.0 * new - old
                    stores.append((flow, j, new))
                    stores.append((change, j, moved))
                    total = total - moved
                stores.append((net, t, total))
            for ref, number, values in stores:
                put(ref, number, values)
            return 0

        lax.fori_loop(0, tiles // UNROLL, one, 0)

    def gather_inner():
        def one(step, _):
            stores = []
            for k in range(UNROLL):
                t = step * UNROLL + k
                total = tile(net, t)
                for group in range(groups):
                    j = group * tiles + lax.rem(t - group + tiles, tiles)
                    total = total + take(tile(change, j), lanes_of(second, blocks + j))
                stores.append((net, t, total))
            for ref, number, values in stores:
                put(ref, number, values)
            return 0

        lax.fori_loop(0, tiles // UNROLL, one, 0)

    def update_cut(tau):
        put(price_far, me_node, tile(price, me_node))

        def one(step, _):
            stores = []
            for k in range(UNROLL):
                t = step * UNROLL + k
                here = tile(price, t)
                other = tile(price_far, t)
                there = take(other, lanes_of(ends_out, t))
                old = tile(cut, t)
                new = jnp.maximum(old - tau * (tile(cost_cut, t) - (there - here)), 0.0)
                stores.append((cut, t, new))
                total = tile(net, t) - (2.0 * new - old)
                there = take(other, lanes_of(ends_in, t))
                old = tile(flow_back, t)
                new = jnp.maximum(old - tau * (tile(cost_back, t) - (here - there)), 0.0)
                stores.append((flow_back, t, new))
                stores.append((net, t, total + (2.0 * new - old)))
            for ref, number, values in stores:
                put(ref, number, values)
            return 0

        lax.fori_loop(0, tiles // UNROLL, one, 0)

    await_rows(got_a, (chunks - 1) * ROWS, recv_sem.at[3])
    chain_back(lambda t: at_period(duals, t), kept, get_summary(got_a, 1), price)
    await_rows(parts, (nodes - 1) * 4, recv_sem.at[5])
    sums = [jnp.sum(parts[pl.ds(row, nodes, stride=ROWS), :], keepdims=True) for row in (0, 2)]
    omega = jnp.sqrt(sums[0] / sums[1])
    tau = jnp.broadcast_to(ETA / omega, (ROWS, LANES))
    sigma = ETA * omega
    sigma_tile = jnp.broadcast_to(sigma, (ROWS, LANES)) * (1.0 / horizon)
    sigma_wide = jnp.broadcast_to(sigma, (tiles, LANES))
    sigma_stock = sigma_wide * (1.0 / horizon)
    update_inner(tau)
    gather_inner()
    await_rows(far_a, (nodes - 1) * 2, recv_sem.at[4])
    chain_back(
        lambda t: packs[pl.ds(3 * ROWS + t, nodes, stride=PACK), :], kept_far, by_node(far_a, 1), price_far
    )
    update_cut(tau)

    def local_stock(target_ref):
        stock = None
        for t in range(ROWS):
            value = by_node(net, t)
            stock = value if stock is None else at_period(kept, t) * stock + value
            value = at_period(duals, t) + sigma_wide * (at_period(targets, t) - stock * (1.0 / horizon))
            duals[pl.ds(t * tiles, tiles), :] = value
            if target_ref is not None:
                target_ref[pl.ds(t, tiles, stride=ROWS), :] = value
        return stock

    put_summary(send_b, 0, local_stock(late))
    put_summary(send_b, 1, passed_back())
    spread_owners(send_b, recv_b, ROWS, 6)
    spread_nodes(late, lates, ROWS, ROWS, 7)
    await_rows(recv_b, (periods - 1) * ROWS, recv_sem.at[6])
    entering = none
    entered = []
    for j in range(periods):
        entered.append(entering)
        entering = tile(recv_b, j) + tile(factor, j) * entering
    entering = none
    for j in reversed(range(periods)):
        put(give_b, j, jnp.where(even, entered[j], entering))
        answer = tile(recv_b, j) - sigma_tile * tile(recv_s, j) * pltpu.roll(entered[j], 1, 0)
        entering = answer + tile(factor, j) * entering
    give_back(give_b, got_b, ROWS, 8)
    give_far(give_b, far_b, 9)

    await_rows(got_b, (chunks - 1) * ROWS, recv_sem.at[8])
    stock = get_summary(got_b, 0) * sigma_stock
    for t in range(ROWS):
        duals[pl.ds(t * tiles, tiles), :] = at_period(duals, t) - at_period(grown, t) * stock
    chain_back(lambda t: at_period(duals, t), kept, get_summary(got_b, 1), price)
    update_inner(tau)
    gather_inner()
    await_rows(lates, (nodes - 1) * ROWS, recv_sem.at[7])
    await_rows(far_b, (nodes - 1) * 2, recv_sem.at[9])
    stock_far = by_node(far_b, 0) * sigma_stock
    chain_back(
        lambda t: by_node(lates, t) - at_period(grown_far, t) * stock_far, kept_far, by_node(far_b, 1), price_far
    )
    update_cut(tau)
    put_summary(send_c, 0, local_stock(None), 1)
    spread_owners(send_c, recv_c, ranks, 10)

    def restore(step, _):
        moved = []
        for k in range(UNROLL):
            t = step * UNROLL + k
            for group in range(groups):
                j = group * tiles + t
                moved.append((flow, j, take(tile(flow, j), lanes_of(tail, j))))
            moved.append((cut, t, take(tile(cut, t), lanes_of(cut_tail, t))))
        for ref, number, values in moved:
            put(ref, number, values)
        return 0

    lax.fori_loop(0, tiles // UNROLL, restore, 0)

    await_rows(recv_c, (periods - 1) * ranks, recv_sem.at[10])
    entering = jnp.zeros((ranks, LANES), jnp.float32)
    for j in range(periods):
        give_c[pl.ds(j * ROWS, ranks), :] = entering
        entering = recv_c[pl.ds(j * ROWS, ranks), :] + factor_c[pl.ds(j * ROWS, ranks), :] * entering
    give_back(give_c, got_c, ranks, 11)
    await_rows(got_c, (chunks - 1) * ranks, recv_sem.at[11])
    stock = get_summary(got_c, 0, 1) * sigma_stock
    for t in range(ROWS):
        dual[pl.ds(t, tiles, stride=ROWS), :] = at_period(duals, t) - at_period(grown, t) * stock

    for phase, rows in (
        (0, (periods - 1) * ROWS),
        (1, (periods - 1) * ROWS),
        (2, (nodes - 1) * SENT),
        (3, (chunks - 1) * ROWS),
        (5, (nodes - 1) * 4),
        (6, (periods - 1) * ROWS),
        (7, (nodes - 1) * ROWS),
        (8, (chunks - 1) * ROWS),
        (10, (periods - 1) * ranks),
        (11, (chunks - 1) * ranks),
    ):
        await_rows(packs, rows, send_sem.at[phase])
    for phase in (4, 9):
        await_rows(packs, chunks * (ranks - 1) * 2, send_sem.at[phase])

        @pl.when(me_chunk != node_chunk)
        def _():
            await_rows(packs, chunks * 2, send_sem.at[phase])


def hand_over(count, *refs):
    semaphores = refs[-1]
    copies = [
        pltpu.make_async_copy(refs[k], refs[count + k], semaphores.at[k]) for k in range(count)
    ]
    for copy in copies:
        copy.start()
    for copy in copies:
        copy.wait()


def solution(mesh):
    nodes, periods = mesh.shape["node"], mesh.shape["period"]

    def to_tiles(values):
        rows, columns = values.shape
        return values.reshape(rows, columns // LANES, LANES).transpose(1, 0, 2).reshape(-1, LANES)

    def from_tiles(values):
        count = values.shape[0] // ROWS
        return values.reshape(count, ROWS, LANES).transpose(1, 0, 2).reshape(ROWS, count * LANES)

    def body(*operands):
        floats = [to_tiles(values) for values in operands[:9]]
        indices = [values.reshape(-1, LANES) for values in operands[9:]]
        tiles = floats[0].shape[0] // ROWS
        groups = floats[1].shape[0] // floats[0].shape[0]
        blocks = tiles * groups
        slab = (tiles * ROWS, LANES)
        arcs = (blocks * ROWS, LANES)
        ring = (periods * ROWS, LANES)
        sorts = (2 * blocks + 2 * nodes, LANES)

        def room(shape, kind=jnp.float32):
            return pltpu.VMEM(shape, kind)

        scratch = [
            room(slab), room(arcs), room(slab), room(slab), room(slab),
            room((blocks, LANES), jnp.int32), room((blocks, LANES), jnp.int32),
            room((tiles, LANES), jnp.int32), room((tiles, LANES), jnp.int32),
            room(slab), room(slab), room(slab), room(slab), room(slab), room(slab),
            room(slab), room(slab), room(slab), room(arcs),
            room(sorts), room(sorts, jnp.int32), room(sorts, jnp.int32),
            room((nodes, LANES), jnp.int32), room((nodes, LANES), jnp.int32),
            room((nodes * PACK, LANES)), room((nodes * PACK, LANES)), room(slab), room(slab),
            room(slab), room(slab), room((ROWS, LANES)), room(slab),
            room(ring), room(ring), room(ring), room(ring), room(slab), room(ring), room(ring),
            room(ring), room(ring), room(ring), room(ring), room(slab),
            room(ring), room(ring), room(ring), room(ring),
            room(ring), room(ring),
            pltpu.SemaphoreType.DMA((13,)),
            pltpu.SemaphoreType.DMA((12,)),
            pltpu.SemaphoreType.DMA((12,)),
        ]
        anywhere = pl.BlockSpec(memory_space=pl.ANY)
        inside = pl.BlockSpec(memory_space=pltpu.VMEM)
        shapes = (slab, arcs, slab, slab)
        results = pl.pallas_call(
            functools.partial(kernel, (nodes, periods, tiles, groups)),
            out_shape=[pltpu.VMEM(shape, jnp.float32) for shape in shapes],
            in_specs=[anywhere] * 13,
            out_specs=[inside] * 4,
            scratch_shapes=scratch,
            compiler_params=pltpu.CompilerParams(
                collective_id=0, has_side_effects=True, vmem_limit_bytes=LIMIT
            ),
        )(*floats, *indices)
        outputs = pl.pallas_call(
            functools.partial(hand_over, 4),
            out_shape=[jax.ShapeDtypeStruct(shape, jnp.float32) for shape in shapes],
            in_specs=[anywhere] * 4,
            out_specs=[anywhere] * 4,
            scratch_shapes=[pltpu.SemaphoreType.DMA((4,))],
            compiler_params=pltpu.CompilerParams(vmem_limit_bytes=LIMIT // 8),
        )(*results)
        return tuple(from_tiles(values) for values in outputs)

    both, node = P("period", "node"), P("node")
    return jax.shard_map(
        body,
        mesh=mesh,
        in_specs=(both,) * 9 + (node,) * 4,
        out_specs=(both,) * 4,
        check_vma=False,
    )
```

time: 97.2 us -> 67.3 us (0.69)
  Pallas kernels: 81.5 us -> 65.6 us
  local copies, waits for them, and re-layouts: 14.5 us -> 0 us
    pallas_call x1, Pallas kernels: 81.5 us -> 64.6 us  [body(): pl.pallas_call(functools.partial(kernel, (nodes, periods, tiles, groups))...]
    unnamed x30 -> x0, local copies, waits for them, and re-layouts: 14.5 us -> none
    pallas_call x0 -> x1, Pallas kernels: none -> 0.99 us  [body(): pl.pallas_call(functools.partial(hand_over, 4), out_shape=[jax.ShapeDtype...]
where the time goes in v2:
time: 67.3 us; the launch traced here: 66.2 us
  Pallas kernels  65.6 us (97%)
    pallas_call x1, Pallas kernels, body(): pl.pallas_call(functools.partial(kernel, (nodes, periods, tiles, groups))...  64.6 us

profile of v2, /device:TPU:1, one launch (start us, length us, event | category | flops | bytes accessed | tf_op | source)
XLA Modules:
  0.0 66.2 jit_solution(4153585972701292571)
XLA Ops:
  0.6 64.6 %shard_map.156 = (f32[256,128]{1,0:T(8,128)S(1)}, f32[1280,128]{1,0:T(8,128)S(1)}, f32[256,128]{1,0:T(8,128)S(1)}, f32[256,128]{1,0:T(8,128)S(1)}) custom-call(f32[256,128]{1,0:T(8,128)} %bitcast.71, f32[1280,128]{1,0:T(8,128)} %bitcast.69, f32[256,128]{1,0:T(8,128)} %bitcast.72, f32[256,128]{1,0:T(8,128)} %bitcast.73, f32[256,128]{1,0:T(8,128)} %bitcast.74, ...), custom_call_target="tpu_custom_call" | custom-call | tf_op jit(solution)/shard_map/pallas_call | solution.py:625
  65.2 1.0 %shard_map.157 = (f32[256,128]{1,0:T(8,128)}, f32[1280,128]{1,0:T(8,128)}, f32[256,128]{1,0:T(8,128)}, f32[256,128]{1,0:T(8,128)}) custom-call(f32[256,128]{1,0:T(8,128)S(1)} %get-tuple-element.12.refs_0_, f32[1280,128]{1,0:T(8,128)S(1)} %get-tuple-element.13.refs_1_, f32[256,128]{1,0:T(8,128)S(1)} %get-tuple-element.14.refs_2_, ...), custom_call_target="tpu_custom_call" | custom-call | tf_op jit(solution)/shard_map/pallas_call | solution.py:635

commit v3 on v2

--- a/solution.py
+++ b/solution.py
@@ -13,7 +13,7 @@
 ROWS = 8
 PACK = 40
 SENT = 34
-UNROLL = 4
+UNROLL = 16
 LIMIT = 56 * 1024 * 1024
 
 
@@ -47,7 +47,7 @@
         price, price_far, net, change,
         keys, second, slot, ends_out, ends_in,
         pack, packs, flow_back, cost_back,
-        late, lates, part, parts,
+        late, lates, part, parts, whole, wholes,
         send_a, recv_a, give_a, got_a, far_a, send_s, recv_s,
         send_b, recv_b, give_b, got_b, far_b,
         send_c, recv_c, give_c, got_c,
@@ -95,20 +95,30 @@
             )
         )
     ]
-    for load in loads:
-        load.start()
-
     def greet(device):
         pl.semaphore_signal(
             pltpu.get_barrier_semaphore(), inc=1, device_id=device, device_id_type=MESH
         )
 
+    def around(i):
+        return lax.rem(
+            me_period + periods // 2 + (1 - 2 * lax.rem(i, 2)) * lax.div(i + 1, 2), periods
+        )
+
+    def away(i):
+        return lax.rem(2 + i + lax.div(i, 2) + 2 * lax.div(i, 3), 4)
+
+    def across(k):
+        y = lax.rem(lax.div(me_node, 8) + away(lax.div(k, 8)), 4)
+        x = lax.rem(lax.div(me_node, 2) + away(lax.rem(lax.div(k, 2), 4)), 4)
+        return y * 8 + x * 2 + lax.rem(me_node + 1 + k, 2)
+
     def greet_period(k, _):
-        greet({"period": lax.rem(me_period + k, periods)})
+        greet({"period": around(k)})
         return 0
 
     def greet_node(k, _):
-        greet({"node": lax.rem(me_node + k, nodes)})
+        greet({"node": across(k)})
         return 0
 
     node_chunk = lax.rem(me_node, chunks)
@@ -117,12 +127,16 @@
     )
 
     def greet_far(k, _):
-        greet({"node": lax.rem(me_node + k, nodes), "period": source_plane})
-        return 0
-
-    lax.fori_loop(1, periods, greet_period, 0)
-    lax.fori_loop(1, nodes, greet_node, 0)
-    lax.fori_loop(1, nodes, greet_far, 0)
+        greet({"node": across(k), "period": source_plane})
+        return 0
+
+    for load in loads[:2]:
+        load.start()
+    lax.fori_loop(0, periods - 1, greet_period, 0)
+    for load in loads[2:]:
+        load.start()
+    lax.fori_loop(0, nodes - 1, greet_far, 0)
+    lax.fori_loop(0, nodes - 1, greet_node, 0)
     far_count = jnp.where(me_chunk == node_chunk, ranks - 1, ranks) * chunks
 
     def start(source, target_ref, source_rows, target_rows, phase, device):
@@ -137,65 +151,61 @@
 
     def spread_owners(source, target_ref, rows, phase):
         def one(k, _):
-            peer = lax.rem(me_period + k, periods)
+            peer = around(k)
             start(
                 source, target_ref, rows_at(lax.rem(peer, chunks), rows), rows_at(me_period, rows), phase,
                 {"period": peer},
             )
             return 0
 
-        lax.fori_loop(1, periods, one, 0)
+        lax.fori_loop(0, periods - 1, one, 0)
         put(target_ref, me_period, tile(source, me_chunk))
 
     def served(i):
-        return lax.rem(me_period + periods - reach + i, periods)
-
-    def give_back(source, target_ref, rows, phase):
+        return lax.rem(
+            me_period + periods - reach + lax.div(i, 2) + lax.rem(i, 2) * (chunks - 1 - 2 * lax.div(i, 2)), periods
+        )
+
+    def give(source, rows, own_ref, phase, far_ref=None, far_phase=None):
         def one(i, _):
-            @pl.when(i != reach)
+            peer = served(i)
+            if far_ref is not None:
+                for rank in range(ranks):
+                    to = me_chunk + rank * chunks
+
+                    @pl.when(to != me_node)
+                    def _():
+                        start(
+                            source, far_ref,
+                            pl.ds(pl.multiple_of(peer * ROWS, ROWS) + 2 * rank, 2), rows_at(me_node, 2), far_phase,
+                            {"node": to, "period": peer},
+                        )
+
+            @pl.when(peer != me_period)
             def _():
-                peer = served(i)
                 start(
-                    source, target_ref, rows_at(peer, rows), rows_at(me_chunk, rows), phase,
-                    {"period": peer},
+                    source, own_ref, rows_at(peer, rows), rows_at(me_chunk, rows), phase, {"period": peer}
                 )
 
             return 0
 
         lax.fori_loop(0, chunks, one, 0)
-        put(target_ref, me_chunk, tile(source, me_period))
-
-    def give_far(source, target_ref, phase):
-        for rank in range(ranks):
-            to = me_chunk + rank * chunks
-
-            @pl.when(to != me_node)
-            def _():
-                def one(i, _):
-                    peer = served(i)
-                    start(
-                        source, target_ref,
-                        pl.ds(pl.multiple_of(peer * ROWS, ROWS) + 2 * rank, 2), rows_at(me_node, 2), phase,
-                        {"node": to, "period": peer},
-                    )
-                    return 0
-
-                lax.fori_loop(0, chunks, one, 0)
+        put(own_ref, me_chunk, tile(source, me_period))
 
     def spread_nodes(source, target_ref, pitch, rows, phase, same=False):
         def one(k, _):
-            peer = lax.rem(me_node + k, nodes)
+            peer = across(k)
             start(
                 source, target_ref, rows_at(0 if same else peer, rows, pitch), rows_at(me_node, rows, pitch), phase,
                 {"node": peer},
             )
             return 0
 
-        lax.fori_loop(1, nodes, one, 0)
+        lax.fori_loop(0, nodes - 1, one, 0)
 
     def await_rows(ref, rows, semaphore):
-        whole = ref.at[pl.ds(0, rows), :]
-        pltpu.make_async_copy(whole, whole, semaphore).wait()
+        span = ref.at[pl.ds(0, rows), :]
+        pltpu.make_async_copy(span, span, semaphore).wait()
 
     def put_summary(ref, row, values, pitch=2):
         for rank in range(ranks):
@@ -288,10 +298,17 @@
         return costs + (first + other), wanted
 
     costs, wanted = lax.fori_loop(0, tiles, square_one, (none, none))
-    put_summary(send_s, 0, jnp.zeros((tiles, LANES), jnp.float32))
-    for row, value in ((0, costs), (2, wanted)):
-        value = jnp.sum(value, axis=0, keepdims=True)
-        send_s[pl.ds(row, chunks, stride=ROWS), :] = jnp.broadcast_to(value, (chunks, LANES))
+    first_row = lax.broadcasted_iota(jnp.int32, (ROWS, LANES), 0) < 1
+    part[...] = jnp.where(
+        first_row, jnp.sum(costs, axis=0, keepdims=True), jnp.sum(wanted, axis=0, keepdims=True)
+    )
+
+    pl.semaphore_wait(pltpu.get_barrier_semaphore(), periods + nodes - 2 + far_count)
+    spread_owners(send_a, recv_a, ROWS, 0)
+    spread_nodes(part, parts, ROWS, 2, 5, same=True)
+    put(parts, me_node, part[...])
+    spread_owners(send_s, recv_s, ROWS, 1)
+    spread_nodes(pack, packs, PACK, SENT, 2)
 
     loads[6].wait()
     loads[7].wait()
@@ -306,7 +323,7 @@
     keys[pl.ds(blocks, blocks), :] = keyed(head[...], tail[...])
     keys[pl.ds(2 * blocks, nodes), :] = keyed(cut_tail[...], cut_head[...])
     keys[pl.ds(2 * blocks + nodes, nodes), :] = keyed(cut_head[...], cut_tail[...])
-    batch = 128
+    batch = 2 * blocks + 2 * nodes
 
     def sort_batch(k, _):
         at = pl.ds(pl.multiple_of(k * batch, batch), batch)
@@ -316,11 +333,6 @@
         return 0
 
     lax.fori_loop(0, (2 * blocks + 2 * nodes) // batch, sort_batch, 0)
-
-    pl.semaphore_wait(pltpu.get_barrier_semaphore(), periods + nodes - 2 + far_count)
-    spread_owners(send_a, recv_a, ROWS, 0)
-    spread_owners(send_s, recv_s, ROWS, 1)
-    spread_nodes(pack, packs, PACK, SENT, 2)
 
     loads[11].wait()
     loads[12].wait()
@@ -345,6 +357,20 @@
     for t in range(ROWS):
         targets[pl.ds(t * tiles, tiles), :] = by_node(target, t)
 
+    await_rows(parts, (nodes - 1) * 2, recv_sem.at[5])
+    whole[...] = jnp.where(
+        first_row,
+        jnp.sum(parts[pl.ds(0, nodes, stride=ROWS), :], axis=0, keepdims=True),
+        jnp.sum(parts[pl.ds(1, nodes, stride=ROWS), :], axis=0, keepdims=True),
+    )
+
+    def spread_whole(k, _):
+        start(whole, wholes, rows_at(0, 2), rows_at(me_period, 2), 12, {"period": around(k)})
+        return 0
+
+    lax.fori_loop(0, periods - 1, spread_whole, 0)
+    put(wholes, me_period, whole[...])
+
     await_rows(recv_a, (periods - 1) * ROWS, recv_sem.at[0])
     entering = none
     for j in reversed(range(periods)):
@@ -353,17 +379,11 @@
         put(factor, j, ratio)
         put(give_a, j, entering)
         entering = block + ratio * entering
-    give_back(give_a, got_a, ROWS, 3)
-    give_far(give_a, far_a, 4)
+    give(give_a, ROWS, got_a, 3, far_a, 4)
 
     await_rows(recv_s, (periods - 1) * ROWS, recv_sem.at[1])
-    total = none
     for j in range(periods):
-        total = total + tile(recv_s, j)
         factor_c[pl.ds(j * ROWS, ranks), :] = factor[pl.ds(j * ROWS, ranks, stride=2), :]
-    part[...] = total
-    spread_nodes(part, parts, ROWS, 4, 5, same=True)
-    put(parts, me_node, total)
 
     await_rows(packs, (nodes - 1) * SENT, recv_sem.at[2])
     packs[rows_at(me_node, PACK, PACK), :] = pack[rows_at(me_node, PACK, PACK), :]
@@ -457,8 +477,8 @@
 
     await_rows(got_a, (chunks - 1) * ROWS, recv_sem.at[3])
     chain_back(lambda t: at_period(duals, t), kept, get_summary(got_a, 1), price)
-    await_rows(parts, (nodes - 1) * 4, recv_sem.at[5])
-    sums = [jnp.sum(parts[pl.ds(row, nodes, stride=ROWS), :], keepdims=True) for row in (0, 2)]
+    await_rows(wholes, (periods - 1) * 2, recv_sem.at[12])
+    sums = [jnp.sum(wholes[pl.ds(row, periods, stride=ROWS), :], keepdims=True) for row in range(2)]
     omega = jnp.sqrt(sums[0] / sums[1])
     tau = jnp.broadcast_to(ETA / omega, (ROWS, LANES))
     sigma = ETA * omega
@@ -499,8 +519,7 @@
         put(give_b, j, jnp.where(even, entered[j], entering))
         answer = tile(recv_b, j) - sigma_tile * tile(recv_s, j) * pltpu.roll(entered[j], 1, 0)
         entering = answer + tile(factor, j) * entering
-    give_back(give_b, got_b, ROWS, 8)
-    give_far(give_b, far_b, 9)
+    give(give_b, ROWS, got_b, 8, far_b, 9)
 
     await_rows(got_b, (chunks - 1) * ROWS, recv_sem.at[8])
     stock = get_summary(got_b, 0) * sigma_stock
@@ -538,7 +557,7 @@
     for j in range(periods):
         give_c[pl.ds(j * ROWS, ranks), :] = entering
         entering = recv_c[pl.ds(j * ROWS, ranks), :] + factor_c[pl.ds(j * ROWS, ranks), :] * entering
-    give_back(give_c, got_c, ranks, 11)
+    give(give_c, ranks, got_c, 11)
     await_rows(got_c, (chunks - 1) * ranks, recv_sem.at[11])
     stock = get_summary(got_c, 0, 1) * sigma_stock
     for t in range(ROWS):
@@ -549,7 +568,8 @@
         (1, (periods - 1) * ROWS),
         (2, (nodes - 1) * SENT),
         (3, (chunks - 1) * ROWS),
-        (5, (nodes - 1) * 4),
+        (5, (nodes - 1) * 2),
+        (12, (periods - 1) * 2),
         (6, (periods - 1) * ROWS),
         (7, (nodes - 1) * ROWS),
         (8, (chunks - 1) * ROWS),
@@ -610,14 +630,14 @@
             room(sorts), room(sorts, jnp.int32), room(sorts, jnp.int32),
             room((nodes, LANES), jnp.int32), room((nodes, LANES), jnp.int32),
             room((nodes * PACK, LANES)), room((nodes * PACK, LANES)), room(slab), room(slab),
-            room(slab), room(slab), room((ROWS, LANES)), room(slab),
+            room(slab), room(slab), room((ROWS, LANES)), room(slab), room((ROWS, LANES)), room(ring),
             room(ring), room(ring), room(ring), room(ring), room(slab), room(ring), room(ring),
             room(ring), room(ring), room(ring), room(ring), room(slab),
             room(ring), room(ring), room(ring), room(ring),
             room(ring), room(ring),
             pltpu.SemaphoreType.DMA((13,)),
-            pltpu.SemaphoreType.DMA((12,)),
-            pltpu.SemaphoreType.DMA((12,)),
+            pltpu.SemaphoreType.DMA((13,)),
+            pltpu.SemaphoreType.DMA((13,)),
         ]
         anywhere = pl.BlockSpec(memory_space=pl.ANY)
         inside = pl.BlockSpec(memory_space=pltpu.VMEM)

time: 67.3 us -> 60.3 us (0.90); the launches traced: 66.2 us -> 60.1 us
  Pallas kernels: 65.6 us -> 59.5 us
    pallas_call x1, Pallas kernels: 64.6 us -> 58.5 us  [body(): pl.pallas_call(functools.partial(kernel, (nodes, periods, tiles, groups))...]
where the time goes in v3:
time: 60.3 us; the launch traced here: 60.1 us
  Pallas kernels  59.5 us (99%)
  between operations  0.64 us (1%)
    pallas_call x1, Pallas kernels, body(): pl.pallas_call(functools.partial(kernel, (nodes, periods, tiles, groups))...  58.5 us

profile of v3, /device:TPU:1, one launch (start us, length us, event | category | flops | bytes accessed | tf_op | source)
XLA Modules:
  0.0 60.1 jit_solution(8421564786236184895)
XLA Ops:
  0.6 58.5 %shard_map.156 = (f32[256,128]{1,0:T(8,128)S(1)}, f32[1280,128]{1,0:T(8,128)S(1)}, f32[256,128]{1,0:T(8,128)S(1)}, f32[256,128]{1,0:T(8,128)S(1)}) custom-call(f32[256,128]{1,0:T(8,128)} %bitcast.71, f32[1280,128]{1,0:T(8,128)} %bitcast.69, f32[256,128]{1,0:T(8,128)} %bitcast.72, f32[256,128]{1,0:T(8,128)} %bitcast.73, f32[256,128]{1,0:T(8,128)} %bitcast.74, ...), custom_call_target="tpu_custom_call" | custom-call | tf_op jit(solution)/shard_map/pallas_call | solution.py:645
  59.1 1.0 %shard_map.157 = (f32[256,128]{1,0:T(8,128)}, f32[1280,128]{1,0:T(8,128)}, f32[256,128]{1,0:T(8,128)}, f32[256,128]{1,0:T(8,128)}) custom-call(f32[256,128]{1,0:T(8,128)S(1)} %get-tuple-element.12.refs_0_, f32[1280,128]{1,0:T(8,128)S(1)} %get-tuple-element.13.refs_1_, f32[256,128]{1,0:T(8,128)S(1)} %get-tuple-element.14.refs_2_, ...), custom_call_target="tpu_custom_call" | custom-call | tf_op jit(solution)/shard_map/pallas_call | solution.py:655

commit v4 on v3

--- a/solution.py
+++ b/solution.py
@@ -122,22 +122,13 @@
         return 0
 
     node_chunk = lax.rem(me_node, chunks)
-    source_plane = node_chunk + chunks * (
-        lax.rem(me_period + periods + reach - node_chunk, periods) // chunks
-    )
-
-    def greet_far(k, _):
-        greet({"node": across(k), "period": source_plane})
-        return 0
 
     for load in loads[:2]:
         load.start()
     lax.fori_loop(0, periods - 1, greet_period, 0)
     for load in loads[2:]:
         load.start()
-    lax.fori_loop(0, nodes - 1, greet_far, 0)
     lax.fori_loop(0, nodes - 1, greet_node, 0)
-    far_count = jnp.where(me_chunk == node_chunk, ranks - 1, ranks) * chunks
 
     def start(source, target_ref, source_rows, target_rows, phase, device):
         pltpu.make_async_remote_copy(
@@ -303,7 +294,7 @@
         first_row, jnp.sum(costs, axis=0, keepdims=True), jnp.sum(wanted, axis=0, keepdims=True)
     )
 
-    pl.semaphore_wait(pltpu.get_barrier_semaphore(), periods + nodes - 2 + far_count)
+    pl.semaphore_wait(pltpu.get_barrier_semaphore(), periods + nodes - 2)
     spread_owners(send_a, recv_a, ROWS, 0)
     spread_nodes(part, parts, ROWS, 2, 5, same=True)
     put(parts, me_node, part[...])
@@ -380,10 +371,6 @@
         put(give_a, j, entering)
         entering = block + ratio * entering
     give(give_a, ROWS, got_a, 3, far_a, 4)
-
-    await_rows(recv_s, (periods - 1) * ROWS, recv_sem.at[1])
-    for j in range(periods):
-        factor_c[pl.ds(j * ROWS, ranks), :] = factor[pl.ds(j * ROWS, ranks, stride=2), :]
 
     await_rows(packs, (nodes - 1) * SENT, recv_sem.at[2])
     packs[rows_at(me_node, PACK, PACK), :] = pack[rows_at(me_node, PACK, PACK), :]
@@ -508,6 +495,10 @@
     put_summary(send_b, 1, passed_back())
     spread_owners(send_b, recv_b, ROWS, 6)
     spread_nodes(late, lates, ROWS, ROWS, 7)
+    await_rows(recv_s, (periods - 1) * ROWS, recv_sem.at[1])
+    for j in range(periods):
+        factor_c[pl.ds(j * ROWS, ranks), :] = factor[pl.ds(j * ROWS, ranks, stride=2), :]
+
     await_rows(recv_b, (periods - 1) * ROWS, recv_sem.at[6])
     entering = none
     entered = []

time: 60.3 us -> 58.8 us (0.975)
  Pallas kernels: 59.5 us -> 57.7 us
    pallas_call x1, Pallas kernels: 58.5 us -> 56.7 us  [body(): pl.pallas_call(functools.partial(kernel, (nodes, periods, tiles, groups))...]
where the time goes in v4:
time: 58.8 us; the launch traced here: 58.3 us
  Pallas kernels  57.7 us (98%)
  between operations  0.64 us (1%)
    pallas_call x1, Pallas kernels, body(): pl.pallas_call(functools.partial(kernel, (nodes, periods, tiles, groups))...  56.7 us

profile of v4, /device:TPU:1, one launch (start us, length us, event | category | flops | bytes accessed | tf_op | source)
XLA Modules:
  0.0 58.3 jit_solution(8480885845148872242)
XLA Ops:
  0.6 56.7 %shard_map.156 = (f32[256,128]{1,0:T(8,128)S(1)}, f32[1280,128]{1,0:T(8,128)S(1)}, f32[256,128]{1,0:T(8,128)S(1)}, f32[256,128]{1,0:T(8,128)S(1)}) custom-call(f32[256,128]{1,0:T(8,128)} %bitcast.71, f32[1280,128]{1,0:T(8,128)} %bitcast.69, f32[256,128]{1,0:T(8,128)} %bitcast.72, f32[256,128]{1,0:T(8,128)} %bitcast.73, f32[256,128]{1,0:T(8,128)} %bitcast.74, ...), custom_call_target="tpu_custom_call" | custom-call | tf_op jit(solution)/shard_map/pallas_call | solution.py:636
  57.3 1.0 %shard_map.157 = (f32[256,128]{1,0:T(8,128)}, f32[1280,128]{1,0:T(8,128)}, f32[256,128]{1,0:T(8,128)}, f32[256,128]{1,0:T(8,128)}) custom-call(f32[256,128]{1,0:T(8,128)S(1)} %get-tuple-element.12.refs_0_, f32[1280,128]{1,0:T(8,128)S(1)} %get-tuple-element.13.refs_1_, f32[256,128]{1,0:T(8,128)S(1)} %get-tuple-element.14.refs_2_, ...), custom_call_target="tpu_custom_call" | custom-call | tf_op jit(solution)/shard_map/pallas_call | solution.py:646

commit v5 on v4

--- a/solution.py
+++ b/solution.py
@@ -52,14 +52,14 @@
         send_b, recv_b, give_b, got_b, far_b,
         send_c, recv_c, give_c, got_c,
         factor, factor_c,
-        in_sem, send_sem, recv_sem,
+        in_sem, send_sem, recv_sem, send_sem_c, recv_sem_c,
     ) = refs
     me_node = lax.axis_index("node")
     me_period = lax.axis_index("period")
     horizon = periods * ROWS
     blocks = groups * tiles
     chunks = periods // 2
-    reach = chunks // 2
+    quarters = chunks // 2
     ranks = tiles // chunks
     me_chunk = lax.rem(me_period, chunks)
 
@@ -140,26 +140,25 @@
             device_id_type=MESH,
         ).start()
 
-    def spread_owners(source, target_ref, rows, phase):
+    def spread_owners(source, target_ref, phase):
         def one(k, _):
             peer = around(k)
             start(
-                source, target_ref, rows_at(lax.rem(peer, chunks), rows), rows_at(me_period, rows), phase,
-                {"period": peer},
+                source, target_ref, rows_at(lax.rem(peer, chunks)), rows_at(me_period), phase, {"period": peer}
             )
             return 0
 
         lax.fori_loop(0, periods - 1, one, 0)
         put(target_ref, me_period, tile(source, me_chunk))
 
-    def served(i):
-        return lax.rem(
-            me_period + periods - reach + lax.div(i, 2) + lax.rem(i, 2) * (chunks - 1 - 2 * lax.div(i, 2)), periods
-        )
-
-    def give(source, rows, own_ref, phase, far_ref=None, far_phase=None):
+    def give(source, count, own_ref, phase, far_ref=None, far_phase=None):
+        place = lax.rem(me_period, count)
+
         def one(i, _):
-            peer = served(i)
+            pair = lax.div(i, 2)
+            peer = lax.rem(
+                me_period + periods - count // 2 + pair + lax.rem(i, 2) * (count - 1 - 2 * pair), periods
+            )
             if far_ref is not None:
                 for rank in range(ranks):
                     to = me_chunk + rank * chunks
@@ -174,14 +173,12 @@
 
             @pl.when(peer != me_period)
             def _():
-                start(
-                    source, own_ref, rows_at(peer, rows), rows_at(me_chunk, rows), phase, {"period": peer}
-                )
+                start(source, own_ref, rows_at(peer), rows_at(place), phase, {"period": peer})
 
             return 0
 
-        lax.fori_loop(0, chunks, one, 0)
-        put(own_ref, me_chunk, tile(source, me_period))
+        lax.fori_loop(0, count, one, 0)
+        put(own_ref, place, tile(source, me_period))
 
     def spread_nodes(source, target_ref, pitch, rows, phase, same=False):
         def one(k, _):
@@ -198,15 +195,22 @@
         span = ref.at[pl.ds(0, rows), :]
         pltpu.make_async_copy(span, span, semaphore).wait()
 
-    def put_summary(ref, row, values, pitch=2):
+    def put_summary(ref, row, values):
         for rank in range(ranks):
-            ref[pl.ds(pitch * rank + row, chunks, stride=ROWS), :] = values[
-                rank * chunks : (rank + 1) * chunks
-            ]
-
-    def get_summary(ref, row, pitch=2):
+            ref[pl.ds(2 * rank + row, chunks, stride=ROWS), :] = values[rank * chunks : (rank + 1) * chunks]
+
+    def get_summary(ref, row):
         return jnp.concatenate(
-            [ref[pl.ds(pitch * rank + row, chunks, stride=ROWS), :] for rank in range(ranks)], axis=0
+            [ref[pl.ds(2 * rank + row, chunks, stride=ROWS), :] for rank in range(ranks)], axis=0
+        )
+
+    def put_quarters(ref, values):
+        for row in range(2 * ranks):
+            ref[pl.ds(row, quarters, stride=ROWS), :] = values[row * quarters : (row + 1) * quarters]
+
+    def get_quarters(ref):
+        return jnp.concatenate(
+            [ref[pl.ds(row, quarters, stride=ROWS), :] for row in range(2 * ranks)], axis=0
         )
 
     def at_period(ref, t):
@@ -252,6 +256,17 @@
     put_summary(send_a, 0, product)
     put_summary(send_a, 1, passed_back())
     put_summary(send_s, 1, square_sum)
+    put_summary(
+        send_s,
+        0,
+        jnp.concatenate(
+            [
+                pltpu.roll(product[rank * chunks : (rank + 1) * chunks], quarters, 0)
+                for rank in range(ranks)
+            ],
+            axis=0,
+        ),
+    )
 
     for k in (2, 3, 4, 5):
         loads[k].wait()
@@ -295,10 +310,10 @@
     )
 
     pl.semaphore_wait(pltpu.get_barrier_semaphore(), periods + nodes - 2)
-    spread_owners(send_a, recv_a, ROWS, 0)
+    spread_owners(send_a, recv_a, 0)
     spread_nodes(part, parts, ROWS, 2, 5, same=True)
     put(parts, me_node, part[...])
-    spread_owners(send_s, recv_s, ROWS, 1)
+    spread_owners(send_s, recv_s, 1)
     spread_nodes(pack, packs, PACK, SENT, 2)
 
     loads[6].wait()
@@ -370,7 +385,7 @@
         put(factor, j, ratio)
         put(give_a, j, entering)
         entering = block + ratio * entering
-    give(give_a, ROWS, got_a, 3, far_a, 4)
+    give(give_a, chunks, got_a, 3, far_a, 4)
 
     await_rows(packs, (nodes - 1) * SENT, recv_sem.at[2])
     packs[rows_at(me_node, PACK, PACK), :] = pack[rows_at(me_node, PACK, PACK), :]
@@ -493,11 +508,14 @@
 
     put_summary(send_b, 0, local_stock(late))
     put_summary(send_b, 1, passed_back())
-    spread_owners(send_b, recv_b, ROWS, 6)
+    spread_owners(send_b, recv_b, 6)
     spread_nodes(late, lates, ROWS, ROWS, 7)
     await_rows(recv_s, (periods - 1) * ROWS, recv_sem.at[1])
     for j in range(periods):
-        factor_c[pl.ds(j * ROWS, ranks), :] = factor[pl.ds(j * ROWS, ranks, stride=2), :]
+        other = tile(recv_s, j)
+        ratio = tile(factor, j)
+        low = jnp.where(even, ratio, pltpu.roll(other, 1, 0))
+        put(factor_c, j, jnp.where(me_chunk < quarters, low, jnp.where(even, other, ratio)))
 
     await_rows(recv_b, (periods - 1) * ROWS, recv_sem.at[6])
     entering = none
@@ -510,7 +528,7 @@
         put(give_b, j, jnp.where(even, entered[j], entering))
         answer = tile(recv_b, j) - sigma_tile * tile(recv_s, j) * pltpu.roll(entered[j], 1, 0)
         entering = answer + tile(factor, j) * entering
-    give(give_b, ROWS, got_b, 8, far_b, 9)
+    give(give_b, chunks, got_b, 8, far_b, 9)
 
     await_rows(got_b, (chunks - 1) * ROWS, recv_sem.at[8])
     stock = get_summary(got_b, 0) * sigma_stock
@@ -526,8 +544,26 @@
         lambda t: by_node(lates, t) - at_period(grown_far, t) * stock_far, kept_far, by_node(far_b, 1), price_far
     )
     update_cut(tau)
-    put_summary(send_c, 0, local_stock(None), 1)
-    spread_owners(send_c, recv_c, ranks, 10)
+    put_quarters(send_c, local_stock(None))
+
+    def spread_later(k, _):
+        peer = around(k)
+
+        @pl.when(jnp.logical_and(me_period < periods - 1, jnp.logical_or(me_period < peer, peer < 2)))
+        def _():
+            pltpu.make_async_remote_copy(
+                src_ref=send_c.at[rows_at(lax.rem(peer, quarters)), :],
+                dst_ref=recv_c.at[rows_at(me_period), :],
+                send_sem=send_sem_c.at[peer],
+                recv_sem=recv_sem_c.at[me_period],
+                device_id={"period": peer},
+                device_id_type=MESH,
+            ).start()
+
+        return 0
+
+    lax.fori_loop(0, periods - 1, spread_later, 0)
+    put(recv_c, me_period, tile(send_c, lax.rem(me_period, quarters)))
 
     def restore(step, _):
         moved = []
@@ -543,14 +579,26 @@
 
     lax.fori_loop(0, tiles // UNROLL, restore, 0)
 
-    await_rows(recv_c, (periods - 1) * ranks, recv_sem.at[10])
-    entering = jnp.zeros((ranks, LANES), jnp.float32)
+    def await_earlier(j, _):
+        @pl.when(
+            jnp.logical_and(
+                jnp.logical_and(j < periods - 1, j != me_period),
+                jnp.logical_or(j < me_period, me_period < 2),
+            )
+        )
+        def _():
+            await_rows(packs, ROWS, recv_sem_c.at[j])
+
+        return 0
+
+    lax.fori_loop(0, periods, await_earlier, 0)
+    entering = none
     for j in range(periods):
-        give_c[pl.ds(j * ROWS, ranks), :] = entering
-        entering = recv_c[pl.ds(j * ROWS, ranks), :] + factor_c[pl.ds(j * ROWS, ranks), :] * entering
-    give(give_c, ranks, got_c, 11)
-    await_rows(got_c, (chunks - 1) * ranks, recv_sem.at[11])
-    stock = get_summary(got_c, 0, 1) * sigma_stock
+        put(give_c, j, entering)
+        entering = tile(recv_c, j) + tile(factor_c, j) * entering
+    give(give_c, quarters, got_c, 11)
+    await_rows(got_c, (quarters - 1) * ROWS, recv_sem.at[11])
+    stock = get_quarters(got_c) * sigma_stock
     for t in range(ROWS):
         dual[pl.ds(t, tiles, stride=ROWS), :] = at_period(duals, t) - at_period(grown, t) * stock
 
@@ -564,10 +612,20 @@
         (6, (periods - 1) * ROWS),
         (7, (nodes - 1) * ROWS),
         (8, (chunks - 1) * ROWS),
-        (10, (periods - 1) * ranks),
-        (11, (chunks - 1) * ranks),
+        (11, (quarters - 1) * ROWS),
     ):
         await_rows(packs, rows, send_sem.at[phase])
+
+    def await_sent(k, _):
+        peer = around(k)
+
+        @pl.when(jnp.logical_and(me_period < periods - 1, jnp.logical_or(me_period < peer, peer < 2)))
+        def _():
+            await_rows(packs, ROWS, send_sem_c.at[peer])
+
+        return 0
+
+    lax.fori_loop(0, periods - 1, await_sent, 0)
     for phase in (4, 9):
         await_rows(packs, chunks * (ranks - 1) * 2, send_sem.at[phase])
 
@@ -629,6 +687,8 @@
             pltpu.SemaphoreType.DMA((13,)),
             pltpu.SemaphoreType.DMA((13,)),
             pltpu.SemaphoreType.DMA((13,)),
+            pltpu.SemaphoreType.DMA((periods,)),
+            pltpu.SemaphoreType.DMA((periods,)),
         ]
         anywhere = pl.BlockSpec(memory_space=pl.ANY)
         inside = pl.BlockSpec(memory_space=pltpu.VMEM)

time: 58.8 us -> 57.5 us (0.978)
  Pallas kernels: 57.7 us -> 56.2 us
    pallas_call x1, Pallas kernels: 56.7 us -> 55.2 us  [body(): pl.pallas_call(functools.partial(kernel, (nodes, periods, tiles, groups))...]
where the time goes in v5:
time: 57.5 us; the launch traced here: 56.8 us
  Pallas kernels  56.2 us (98%)
  between operations  0.64 us (1%)
    pallas_call x1, Pallas kernels, body(): pl.pallas_call(functools.partial(kernel, (nodes, periods, tiles, groups))...  55.2 us

profile of v5, /device:TPU:1, one launch (start us, length us, event | category | flops | bytes accessed | tf_op | source)
XLA Modules:
  0.0 56.8 jit_solution(2397246016491696089)
XLA Ops:
  0.6 55.2 %shard_map.156 = (f32[256,128]{1,0:T(8,128)S(1)}, f32[1280,128]{1,0:T(8,128)S(1)}, f32[256,128]{1,0:T(8,128)S(1)}, f32[256,128]{1,0:T(8,128)S(1)}) custom-call(f32[256,128]{1,0:T(8,128)} %bitcast.71, f32[1280,128]{1,0:T(8,128)} %bitcast.69, f32[256,128]{1,0:T(8,128)} %bitcast.72, f32[256,128]{1,0:T(8,128)} %bitcast.73, f32[256,128]{1,0:T(8,128)} %bitcast.74, ...), custom_call_target="tpu_custom_call" | custom-call | tf_op jit(solution)/shard_map/pallas_call | solution.py:696
  55.8 1.0 %shard_map.157 = (f32[256,128]{1,0:T(8,128)}, f32[1280,128]{1,0:T(8,128)}, f32[256,128]{1,0:T(8,128)}, f32[256,128]{1,0:T(8,128)}) custom-call(f32[256,128]{1,0:T(8,128)S(1)} %get-tuple-element.12.refs_0_, f32[1280,128]{1,0:T(8,128)S(1)} %get-tuple-element.13.refs_1_, f32[256,128]{1,0:T(8,128)S(1)} %get-tuple-element.14.refs_2_, ...), custom_call_target="tpu_custom_call" | custom-call | tf_op jit(solution)/shard_map/pallas_call | solution.py:706

commit v6 on v5

--- a/solution.py
+++ b/solution.py
@@ -313,7 +313,6 @@
     spread_owners(send_a, recv_a, 0)
     spread_nodes(part, parts, ROWS, 2, 5, same=True)
     put(parts, me_node, part[...])
-    spread_owners(send_s, recv_s, 1)
     spread_nodes(pack, packs, PACK, SENT, 2)
 
     loads[6].wait()
@@ -479,6 +478,7 @@
 
     await_rows(got_a, (chunks - 1) * ROWS, recv_sem.at[3])
     chain_back(lambda t: at_period(duals, t), kept, get_summary(got_a, 1), price)
+    spread_owners(send_s, recv_s, 1)
     await_rows(wholes, (periods - 1) * 2, recv_sem.at[12])
     sums = [jnp.sum(wholes[pl.ds(row, periods, stride=ROWS), :], keepdims=True) for row in range(2)]
     omega = jnp.sqrt(sums[0] / sums[1])

time: 57.5 us -> 58.8 us (1.023)
  Pallas kernels: 56.2 us -> 58 us
    pallas_call x1, Pallas kernels: 55.2 us -> 57 us  [body(): pl.pallas_call(functools.partial(kernel, (nodes, periods, tiles, groups))...]
where the time goes in v6:
time: 58.8 us; the launch traced here: 58.7 us
  Pallas kernels  58 us (99%)
  between operations  0.64 us (1%)
    pallas_call x1, Pallas kernels, body(): pl.pallas_call(functools.partial(kernel, (nodes, periods, tiles, groups))...  57 us

profile of v6, /device:TPU:1, one launch (start us, length us, event | category | flops | bytes accessed | tf_op | source)
XLA Modules:
  0.0 58.7 jit_solution(5465711401080791792)
XLA Ops:
  0.6 57.0 %shard_map.156 = (f32[256,128]{1,0:T(8,128)S(1)}, f32[1280,128]{1,0:T(8,128)S(1)}, f32[256,128]{1,0:T(8,128)S(1)}, f32[256,128]{1,0:T(8,128)S(1)}) custom-call(f32[256,128]{1,0:T(8,128)} %bitcast.71, f32[1280,128]{1,0:T(8,128)} %bitcast.69, f32[256,128]{1,0:T(8,128)} %bitcast.72, f32[256,128]{1,0:T(8,128)} %bitcast.73, f32[256,128]{1,0:T(8,128)} %bitcast.74, ...), custom_call_target="tpu_custom_call" | custom-call | tf_op jit(solution)/shard_map/pallas_call | solution.py:696
  57.7 1.0 %shard_map.157 = (f32[256,128]{1,0:T(8,128)}, f32[1280,128]{1,0:T(8,128)}, f32[256,128]{1,0:T(8,128)}, f32[256,128]{1,0:T(8,128)}) custom-call(f32[256,128]{1,0:T(8,128)S(1)} %get-tuple-element.12.refs_0_, f32[1280,128]{1,0:T(8,128)S(1)} %get-tuple-element.13.refs_1_, f32[256,128]{1,0:T(8,128)S(1)} %get-tuple-element.14.refs_2_, ...), custom_call_target="tpu_custom_call" | custom-call | tf_op jit(solution)/shard_map/pallas_call | solution.py:706
